TPU v7x, 32 devices: a whole 2x2x4 slice. The times are simulated.
32 devices in a mesh: items: 8 (over z, x), ffn: 4 (over y, core).
Axes of the slice: x: 2, y: 2, z: 4, core: 2. Of those that a mesh axis runs over, the one named last changes fastest.
Arguments:
- text_rows: bfloat16 [32, 4, 502, 768], P(('items', 'ffn')), may hold values from -6 to 6
- attn_weight: bfloat16 [3072, 768], P(('items', 'ffn'))
- vectors: bfloat16 [18, 768], P(None, ('items', 'ffn'))
- w_in: bfloat16 [768, 3072], P('items', 'ffn'), may hold values from -0.21875 to 0.21875
- b_in: bfloat16 [4, 768], P('ffn', 'items'), may hold values from -1.5 to 1.5
- w_out: bfloat16 [3072, 768], P('ffn', 'items'), may hold values from -0.109375 to 0.109375
- seg_count: int32 [32], P(('items', 'ffn')), may hold values from 2 to 4, as said below
- last_fill: int32 [32], P(('items', 'ffn')), may hold values from 1 to 502, as said below
- out_grad: bfloat16 [32, 4, 502, 768], P(('items', 'ffn')), may hold values from -6 to 6
- mem_grad: float32 [32, 10, 768], P(('items', 'ffn')), may hold values from -6 to 6
Outputs:
- activations: bfloat16 [32, 4, 502, 768], P(('items', 'ffn'))
- final_memory: float32 [32, 10, 768], P(('items', 'ffn'))
- text_grad: float32 [32, 4, 502, 768], P(('items', 'ffn'))
- attn_grad: float32 [3072, 768], P(('items', 'ffn'))
- vector_grad: float32 [18, 768], P(None, ('items', 'ffn'))
- w_in_grad: float32 [768, 3072], P('items', 'ffn')
- b_in_grad: float32 [4, 768], P('ffn', 'items')
- w_out_grad: float32 [3072, 768], P('ffn', 'items')
Inputs may be any that keep to these rules, and one draw needn't show every extreme that they name: `seg_count`: some item has 4 segments. `last_fill`: some item's last segment is full.
All inputs are finite; a program needn't handle non-finite values.
Results may differ from a plain program's by a relative error of at most 0.025.
Values may be sent and summed in bfloat16 or wider, within the bound.
No kernel may reach another device: no remote copies, remote signals or barrier semaphores. Data moves between devices by JAX's collectives and lax.ppermute only.
A program may use at most 384 MiB of HBM per device.

v0:
```python
import functools

import jax
import jax.numpy as jnp
from jax import lax
from jax.experimental import pallas as pl
from jax.experimental.layout import Layout, with_layout_constraint
from jax.experimental.pallas import tpu as pltpu
from jax.sharding import PartitionSpec as P

HEADS = 12
HD = 64
MEM = 10
TEXT = 502
SEGS_MAX = 4
ROWS = TEXT + MEM
AUG = 16

epsilon = 1e-12
root_half = 0.7071067811865476
inv_root_tau = 0.3989422804014327
log_two = 0.6931471805599453

f32 = jnp.float32
bf16 = jnp.bfloat16
AXES = ("items", "ffn")


def dot_nn(a, b):
    return jnp.dot(a, b, preferred_element_type=f32)


def dot_nt(a, b):
    return lax.dot_general(a, b, (((1,), (1,)), ((), ())), preferred_element_type=f32)


def dot_tn(a, b):
    return lax.dot_general(a, b, (((0,), (0,)), ((), ())), preferred_element_type=f32)


def split_three(value):
    high = value.astype(bf16)
    rest = value - high.astype(f32)
    mid = rest.astype(bf16)
    last = (rest - mid.astype(f32)).astype(bf16)
    return high, mid, last


def gelu_both(pre):
    half = 0.5 * (1.0 + lax.erf(pre * root_half))
    slope = half + pre * jnp.exp(-0.5 * pre * pre) * inv_root_tau
    return pre * half, slope


def norm_rows(value):
    centered = value - jnp.mean(value, axis=-1, keepdims=True)
    inverse = lax.rsqrt(jnp.mean(centered * centered, axis=-1, keepdims=True) + epsilon)
    return centered * inverse, inverse


def norm_rows_back(upstream, normed, inverse, gain):
    scaled = upstream * gain
    return inverse * (
        scaled
        - jnp.mean(scaled, axis=-1, keepdims=True)
        - normed * jnp.mean(scaled * normed, axis=-1, keepdims=True)
    )


def fill_limit(seg, count, fill):
    return jnp.where(seg < count, jnp.where(seg == count - 1, fill, TEXT), 0)


def aug_rows(first, second):
    width = first[0].shape[1]
    row = lax.broadcasted_iota(jnp.int32, (AUG, width), 0)
    out = jnp.zeros((AUG, width), f32)
    for place, piece in enumerate(tuple(first) + tuple(second)):
        out = jnp.where(row == place, jnp.broadcast_to(piece.astype(f32), (AUG, width)), out)
    return out.astype(bf16)


def ones_three(width):
    one = jnp.ones((1, width), bf16)
    return (one, one, one)


def key_bias(limit):
    place = lax.broadcasted_iota(jnp.int32, (1, ROWS), 1)
    bias = jnp.where(place < limit, 0.0, jnp.where(place < TEXT, -1e9, log_two)).astype(f32)
    return split_three(bias)


def start_loads(table_ref, pieces, plan, targets, sems, wanted):
    for place, (piece, start, rows, target) in enumerate(plan):
        if target not in wanted:
            continue
        dest = pl.multiple_of(table_ref[place], rows)
        pltpu.make_async_copy(
            pieces[piece].at[pl.ds(start, rows), :], targets[target].at[pl.ds(dest, rows), :], sems.at[target]
        ).start()


def wait_loads(targets, sems, target):
    pltpu.make_async_copy(targets[target], targets[target], sems.at[target]).wait()


def early_kernel(plan, n_pieces, count_ref, fill_ref, table_ref, text_ref, col_ref, *refs):
    pieces = refs[:n_pieces]
    qkv_ref, mean_ref, lse_ref, z_ref, attn_ref, turned_ref, sems = refs[n_pieces:]
    seg = pl.program_id(0)
    limit = fill_limit(seg, count_ref[0], fill_ref[0])
    width = z_ref.shape[1]

    @pl.when(seg == 0)
    def _():
        start_loads(table_ref, pieces, plan, (attn_ref,), sems, (0,))
        z_ref[...] = jnp.zeros_like(z_ref)
        wait_loads((attn_ref,), sems, 0)
        for c in range(3):
            turned_ref[c * width : (c + 1) * width, :] = attn_ref[c * width : (c + 1) * width, :].T

    z_ref[:TEXT, :] = text_ref[0].astype(f32)
    zl = z_ref[...].astype(bf16)
    lane = lax.broadcasted_iota(jnp.int32, (1, ROWS), 1)
    for c in range(3):
        part = dot_nt(turned_ref[c * width : (c + 1) * width, :], zl)
        if c != 1:
            part = part + col_ref[:, c // 2 : c // 2 + 1]
        part = jnp.where(lane < TEXT, part, 0.0).astype(bf16)
        if c == 0:
            part = part * jnp.asarray(HD ** (-0.5), bf16)
        qkv_ref[c * width : (c + 1) * width, :] = part

    ones = ones_three(ROWS)
    key_aug = aug_rows(split_three(jnp.where(lane < limit, 0.0, -1e9).astype(f32)), ())
    query_aug = aug_rows(ones, ())

    def scores_of(head):
        lo = head * HD
        q_aug = jnp.concatenate([qkv_ref[lo : lo + HD, :], query_aug], axis=0)
        k_aug = jnp.concatenate([qkv_ref[width + lo : width + lo + HD, :], key_aug], axis=0)
        return dot_tn(k_aug, q_aug)

    def mix(head, peak, expo):
        lo = head * HD
        v_aug = jnp.concatenate([qkv_ref[2 * width + lo : 2 * width + lo + HD, :], query_aug], axis=0)
        both = dot_nn(v_aug, expo)
        total = both[HD : HD + 1, :]
        mean_ref[lo : lo + HD, :] = jnp.where(lane < TEXT, both[:HD, :] * (1.0 / total), 0.0).astype(bf16)
        lse_ref[0, head : head + 1, :] = jnp.where(lane < TEXT, peak + jnp.log(total), 0.0)

    lse_ref[...] = jnp.zeros_like(lse_ref)
    scores, held = scores_of(0), None
    for head in range(HEADS):
        following = scores_of(head + 1) if head + 1 < HEADS else None
        if held is not None:
            mix(head - 1, *held)
        peak = jnp.max(scores, axis=0, keepdims=True)
        held = peak, jnp.exp(scores - peak).astype(bf16)
        scores = following
    mix(HEADS - 1, *held)


def early_call(count, fill, text, col, table, plan, pieces):
    width = text.shape[-1]
    total = SEGS_MAX * ROWS

    def lanes(height):
        return pl.BlockSpec((height, ROWS), lambda s: (0, s))

    sds = jax.ShapeDtypeStruct
    return pl.pallas_call(
        functools.partial(early_kernel, plan, len(pieces)),
        grid=(SEGS_MAX,),
        in_specs=[scalar(), scalar(), scalar(), pl.BlockSpec((1, TEXT, width), lambda s: (s, 0, 0)), whole()]
        + [remain()] * len(pieces),
        out_specs=[lanes(3 * width), lanes(width), pl.BlockSpec((1, 16, ROWS), lambda s: (s, 0, 0))],
        out_shape=[sds((3 * width, total), bf16), sds((width, total), bf16), sds((SEGS_MAX, 16, ROWS), f32)],
        scratch_shapes=[
            pltpu.VMEM((ROWS, width), f32), pltpu.VMEM((4 * width, width), bf16),
            pltpu.VMEM((3 * width, width), bf16), pltpu.SemaphoreType.DMA((1,)),
        ],
        compiler_params=pltpu.CompilerParams(vmem_limit_bytes=62 * 2**20),
    )(count, fill, table, text, col, *pieces)


def forward_kernel(
    plan, n_pieces, count_ref, fill_ref, table_ref, text_ref, bin_ref, vec_ref, *refs,
):
    early, pieces, refs = refs[:3], refs[3 : 3 + n_pieces], refs[3 + n_pieces :]
    forward_segment(plan, pieces, count_ref, fill_ref, table_ref, text_ref, bin_ref, vec_ref, *early, *refs)


def forward_segment(
    plan, pieces, count_ref, fill_ref, table_ref, text_ref, bin_ref, vec_ref, text_qkv_ref, mean_ref, text_lse_ref,
    out_ref, mem_ref, zl_ref, qkv_ref, mixed_ref, lse_ref, n1_ref, r1_ref, hl_ref, act_ref,
    slope_ref, n2_ref, r2_ref,
    memory, z_ref, h_ref, acc_ref, attn_ref, win_ref, wout_ref, sems,
):
    weights = (attn_ref, win_ref, wout_ref)
    seg = pl.program_id(0)
    count, fill = count_ref[0], fill_ref[0]
    limit = fill_limit(seg, count, fill)
    width = z_ref.shape[1]

    @pl.when(seg == 0)
    def _():
        start_loads(table_ref, pieces, plan, weights, sems, (0,))
        memory[...] = jnp.zeros_like(memory)
        memory[:MEM, :] = vec_ref[8 : 8 + MEM, :]
        wait_loads(weights, sems, 0)
        start_loads(table_ref, pieces, plan, weights, sems, (1, 2))

    z_ref[:TEXT, :] = text_ref[0].astype(f32)
    z_ref[TEXT:, :] = memory[:MEM, :]
    zl_ref[...] = z_ref[...].astype(bf16)

    edge = ROWS - 128
    low = memory[...].astype(bf16)
    row = lax.broadcasted_iota(jnp.int32, (AUG, 1), 0)
    spots = lax.broadcasted_iota(jnp.int32, (AUG, 128), 1) == row + (TEXT - edge)
    spots = jnp.where(spots & (row < MEM), 1.0, 0.0).astype(bf16)
    few = []
    for c in range(3):
        part = dot_nn(low, attn_ref[c * width : (c + 1) * width, :])
        if c != 1:
            part = part + vec_ref[c // 2 : c // 2 + 1, :]
        part = jnp.where(row < MEM, part, 0.0).astype(bf16)
        if c == 0:
            part = part * jnp.asarray(HD ** (-0.5), bf16)
        few.append(part)
        rows = slice(c * width, (c + 1) * width)
        qkv_ref[rows, :edge] = text_qkv_ref[rows, :edge]
        qkv_ref[rows, edge:] = (text_qkv_ref[rows, edge:].astype(f32) + dot_tn(part, spots)).astype(bf16)

    tall = (HEADS * AUG, 1)
    tall_row = lax.broadcasted_iota(jnp.int32, tall, 0)
    its_head = (tall_row >> 4) == (lax.broadcasted_iota(jnp.int32, (1, width), 1) >> 6)
    its_row = tall_row & 15

    def by_head(value):
        value = jnp.concatenate([value.astype(f32)] * HEADS, axis=0)
        return jnp.where(its_head, value, 0.0).astype(bf16)

    q_few, k_few, v_few = (by_head(part) for part in few)

    lane = lax.broadcasted_iota(jnp.int32, (1, ROWS), 1)
    scores = dot_nn(q_few, text_qkv_ref[width : 2 * width, :]) + jnp.where(lane < limit, 0.0, -1e9)
    peak = jnp.max(scores, axis=1, keepdims=True)
    expo = jnp.exp(scores - peak)
    total = jnp.sum(expo, axis=1, keepdims=True)
    mean = dot_nt((expo / total).astype(bf16), text_qkv_ref[2 * width :, :])
    mean = jnp.sum(jnp.where(its_head, mean, 0.0).reshape(HEADS, AUG, width), axis=0).astype(bf16)
    mean_edge = mean_ref[:, edge:].astype(f32) + dot_tn(mean, spots)
    head_lane = lax.broadcasted_iota(jnp.int32, (1, AUG), 1)
    spread = jnp.where((tall_row >> 4) == head_lane, peak + jnp.log(total), 0.0)
    tall_spots = lax.broadcasted_iota(jnp.int32, (HEADS * AUG, 128), 1) == its_row + (TEXT - edge)
    tall_spots = jnp.where(tall_spots & (its_row < MEM), 1.0, 0.0).astype(bf16)
    lse_ref[0, :, :edge] = text_lse_ref[0, :, :edge]
    lse_ref[0, :, edge:] = text_lse_ref[0, :, edge:] + sum(dot_tn(piece, tall_spots) for piece in split_three(spread))

    scores = dot_nn(k_few, qkv_ref[:width, :]) + jnp.where(its_row < MEM, log_two, -1e9)
    scores = scores.reshape(HEADS, AUG, ROWS)
    text_lse = lse_ref[0, :HEADS, :]
    peak = jnp.maximum(text_lse, jnp.max(scores, axis=1))
    expo = jnp.exp(scores - peak[:, None, :])
    text_part = jnp.exp(text_lse - peak)
    total = text_part + jnp.sum(expo, axis=1)
    inverse = 1.0 / total
    lse_ref[0, :HEADS, :] = peak + jnp.log(total)
    text_part = text_part * inverse
    expo = (expo * inverse[:, None, :]).reshape(HEADS * AUG, ROWS).astype(bf16)
    extra = dot_tn(v_few, expo)
    for head in range(HEADS):
        rows = slice(head * HD, (head + 1) * HD)
        share = text_part[head : head + 1, :]
        mixed_ref[rows, :edge] = (mean_ref[rows, :edge].astype(f32) * share[:, :edge] + extra[rows, :edge]).astype(bf16)
        mixed_ref[rows, edge:] = (mean_edge[rows, :] * share[:, edge:] + extra[rows, edge:]).astype(bf16)

    first = z_ref[...] + (dot_tn(mixed_ref[...], attn_ref[3 * width :, :]) + vec_ref[2:3, :])
    normed, inverse = norm_rows(first)
    n1_ref[...] = normed.astype(bf16)
    r1_ref[...] = inverse
    h = normed * vec_ref[3:4, :] + vec_ref[4:5, :]
    h_ref[...] = h
    hl_ref[...] = h.astype(bf16)

    @pl.when(seg == 0)
    def _():
        wait_loads(weights, sems, 1)
        wait_loads(weights, sems, 2)

    blocks, block = bin_ref.shape
    for low in range(0, ROWS, ROWS // 2):
        rs = slice(low, low + ROWS // 2)
        for f in range(blocks):
            sl, cs = slice(f * width, (f + 1) * width), slice(f * block, (f + 1) * block)
            pre = dot_nn(hl_ref[rs, :], win_ref[sl, :]) + bin_ref[f : f + 1, :]
            act, slope = gelu_both(pre)
            act_ref[rs, cs] = act.astype(bf16)
            slope_ref[rs, cs] = slope.astype(bf16)
        part = dot_nt(act_ref[rs, :block], wout_ref[:width, :])
        for f in range(1, blocks):
            part += dot_nt(act_ref[rs, f * block : (f + 1) * block], wout_ref[f * width : (f + 1) * width, :])
        acc_ref[rs, :] = part

    normed, inverse = norm_rows(h_ref[...] + (acc_ref[...] + vec_ref[5:6, :]))
    n2_ref[...] = normed.astype(bf16)
    r2_ref[...] = inverse
    y = normed * vec_ref[6:7, :] + vec_ref[7:8, :]
    row = lax.broadcasted_iota(jnp.int32, (TEXT, 1), 0)
    out_ref[0] = jnp.where(row < limit, y[:TEXT, :], 0.0).astype(bf16)
    memory[:MEM, :] = jnp.where(seg < count, y[TEXT:, :], memory[:MEM, :])
    mem_ref[...] = memory[:MEM, :]


def backward_kernel(
    plan, n_pieces, count_ref, fill_ref, table_ref, grad_ref, mgrad_ref, vec_ref, *refs,
):
    pieces, refs = refs[:n_pieces], refs[n_pieces:]
    backward_segment(plan, pieces, count_ref, fill_ref, table_ref, grad_ref, mgrad_ref, vec_ref, *refs)


def backward_segment(
    plan, pieces, count_ref, fill_ref, table_ref, grad_ref, mgrad_ref, vec_ref,
    qkv_ref, mixed_ref, lse_ref, n1_ref, r1_ref, slope_ref, n2_ref, r2_ref,
    first_ref, gbranch_ref, gpre_ref, gattn_ref, gqkv_ref, vgrad_ref, bgrad_ref, gmem_ref,
    edge_ref, gm_ref, gy_ref, second_ref, acc_ref, mix_ref, cols_ref, attn_ref, win_ref, wout_ref, sems,
):
    weights = (attn_ref, win_ref, wout_ref)
    step = pl.program_id(0)
    seg = SEGS_MAX - 1 - step
    count, fill = count_ref[0], fill_ref[0]
    limit = fill_limit(seg, count, fill)
    width = gy_ref.shape[1]

    @pl.when(step == 0)
    def _():
        start_loads(table_ref, pieces, plan, weights, sems, (1, 2))
        gm_ref[...] = mgrad_ref[0]
        vgrad_ref[...] = jnp.zeros_like(vgrad_ref)
        bgrad_ref[...] = jnp.zeros_like(bgrad_ref)

    row = lax.broadcasted_iota(jnp.int32, (TEXT, 1), 0)
    gy_ref[:TEXT, :] = jnp.where(row < limit, grad_ref[0].astype(f32), 0.0)
    gy_ref[TEXT:, :] = jnp.where(seg < count, gm_ref[...], 0.0)

    def column_sum(value):
        return jnp.sum(value, axis=0, keepdims=True)

    gy = gy_ref[...]
    normed = n2_ref[...].astype(f32)
    vgrad_ref[6:7, :] += column_sum(gy * normed)
    vgrad_ref[7:8, :] += column_sum(gy)
    second = norm_rows_back(gy, normed, r2_ref[...], vec_ref[6:7, :])
    second_ref[...] = second
    gbranch_ref[...] = second.astype(bf16)
    vgrad_ref[5:6, :] += column_sum(gbranch_ref[...].astype(f32))

    @pl.when(step == 0)
    def _():
        wait_loads(weights, sems, 2)
        wait_loads(weights, sems, 1)
        start_loads(table_ref, pieces, plan, weights, sems, (0,))

    blocks, block = bgrad_ref.shape
    for f in range(blocks):
        sl = slice(f * block, (f + 1) * block)
        rows = slice(f * width, (f + 1) * width)
        hidden = dot_nn(gbranch_ref[...], wout_ref[rows, :])
        pre = (hidden * slope_ref[:, sl].astype(f32)).astype(bf16)
        gpre_ref[:, sl] = pre
        bgrad_ref[f : f + 1, :] += column_sum(pre.astype(f32))
        part = dot_nt(gpre_ref[:, sl], win_ref[rows, :])
        if f == 0:
            acc_ref[...] = part
        else:
            acc_ref[...] += part

    gh = second_ref[...] + acc_ref[...]
    normed = n1_ref[...].astype(f32)
    vgrad_ref[3:4, :] += column_sum(gh * normed)
    vgrad_ref[4:5, :] += column_sum(gh)
    first = norm_rows_back(gh, normed, r1_ref[...], vec_ref[3:4, :])
    second_ref[...] = first
    gattn_ref[...] = first.astype(bf16)
    vgrad_ref[2:3, :] += column_sum(gattn_ref[...].astype(f32))

    @pl.when(step == 0)
    def _():
        wait_loads(weights, sems, 0)

    mix_ref[...] = dot_nt(attn_ref[3 * width :, :], gattn_ref[...]).astype(bf16)

    ones = ones_three(ROWS)
    key_aug = aug_rows(key_bias(limit), ones)
    value_aug = aug_rows(ones, ())

    def maps_of(head):
        lo = head * HD
        q_h = qkv_ref[lo : lo + HD, :]
        k_h = qkv_ref[width + lo : width + lo + HD, :]
        v_h = qkv_ref[2 * width + lo : 2 * width + lo + HD, :]
        g_h = mix_ref[lo : lo + HD, :]
        inner = column_sum(g_h.astype(f32) * mixed_ref[lo : lo + HD, :].astype(f32))
        q_aug = jnp.concatenate([q_h, aug_rows(ones, split_three(-lse_ref[0, head : head + 1, :]))], axis=0)
        k_aug = jnp.concatenate([k_h, key_aug], axis=0)
        v_aug = jnp.concatenate([v_h, value_aug], axis=0)
        g_aug = jnp.concatenate([g_h, aug_rows(split_three(-inner), ())], axis=0)
        return dot_tn(q_aug, k_aug), dot_tn(g_aug, v_aug)

    def spread(head, grads, probs):
        lo = head * HD
        cols_ref[lo : lo + HD, :] = dot_nt(qkv_ref[width + lo : width + lo + HD, :], grads) * (HD ** (-0.5))
        cols_ref[width + lo : width + lo + HD, :] = dot_nn(qkv_ref[lo : lo + HD, :], grads)
        cols_ref[2 * width + lo : 2 * width + lo + HD, :] = dot_nn(mix_ref[lo : lo + HD, :], probs)

    maps = maps_of(0)
    for head in range(HEADS):
        following = maps_of(head + 1) if head + 1 < HEADS else None
        probs = jnp.exp(maps[0])
        spread(head, (probs * maps[1]).astype(bf16), probs.astype(bf16))
        maps = following

    for c in range(3):
        gqkv_ref[:, c * width : (c + 1) * width] = cols_ref[c * width : (c + 1) * width, :].T.astype(bf16)
    vgrad_ref[0:1, :] += column_sum(gqkv_ref[:, :width].astype(f32))
    vgrad_ref[1:2, :] += column_sum(gqkv_ref[:, 2 * width :].astype(f32))
    first_ref[...] = second_ref[...]
    edge = ROWS - AUG
    joined = second_ref[edge:, :]
    for c in range(3):
        joined = joined + dot_nt(gqkv_ref[edge:, c * width : (c + 1) * width], attn_ref[c * width : (c + 1) * width, :])
    edge_ref[...] = joined
    gm_ref[...] = jnp.where(seg < count, edge_ref[AUG - MEM :, :], gm_ref[...])
    gmem_ref[...] = gm_ref[...]


def whole():
    return pl.BlockSpec(memory_space=pltpu.VMEM)


def scalar():
    return pl.BlockSpec(memory_space=pltpu.SMEM)


def remain():
    return pl.BlockSpec(memory_space=pl.ANY)


def weight_scratch(width, blocks, block):
    return [
        pltpu.VMEM((4 * width, width), bf16), pltpu.VMEM((blocks * width, block), bf16),
        pltpu.VMEM((blocks * width, block), bf16),
    ]


def forward_call(count, fill, text, bias, vec, early, table, plan, pieces):
    width = text.shape[-1]
    blocks, block = bias.shape
    hidden = blocks * block
    total = SEGS_MAX * ROWS

    def rows(cols):
        return pl.BlockSpec((ROWS, cols), lambda s: (s, 0))

    def lanes(height):
        return pl.BlockSpec((height, ROWS), lambda s: (0, s))

    seg_block = pl.BlockSpec((1, TEXT, width), lambda s: (s, 0, 0))
    sds = jax.ShapeDtypeStruct
    return pl.pallas_call(
        functools.partial(forward_kernel, plan, len(pieces)),
        grid=(SEGS_MAX,),
        in_specs=[scalar(), scalar(), scalar(), seg_block] + [whole()] * 2
        + [lanes(3 * width), lanes(width), pl.BlockSpec((1, 16, ROWS), lambda s: (s, 0, 0))]
        + [remain()] * len(pieces),
        out_specs=[
            seg_block, pl.BlockSpec((MEM, width), lambda s: (0, 0)),
            rows(width), lanes(3 * width), lanes(width),
            pl.BlockSpec((1, 16, ROWS), lambda s: (s, 0, 0)),
            rows(width), rows(1), rows(width), rows(hidden), rows(hidden), rows(width), rows(1),
        ],
        out_shape=[
            sds((SEGS_MAX, TEXT, width), bf16), sds((MEM, width), f32),
            sds((total, width), bf16), sds((3 * width, total), bf16), sds((width, total), bf16),
            sds((SEGS_MAX, 16, ROWS), f32),
            sds((total, width), bf16), sds((total, 1), f32), sds((total, width), bf16),
            sds((total, hidden), bf16), sds((total, hidden), bf16), sds((total, width), bf16),
            sds((total, 1), f32),
        ],
        scratch_shapes=[
            pltpu.VMEM((AUG, width), f32), pltpu.VMEM((ROWS, width), f32),
            pltpu.VMEM((ROWS, width), f32), pltpu.VMEM((ROWS, width), f32),
        ]
        + weight_scratch(width, blocks, block)
        + [pltpu.SemaphoreType.DMA((3,))],
        compiler_params=pltpu.CompilerParams(vmem_limit_bytes=62 * 2**20),
    )(count, fill, table, text, bias, vec, *early, *pieces)


def backward_call(count, fill, out_grad, mem_grad, vec, saved, shape, table, plan, pieces):
    width = out_grad.shape[-1]
    blocks, block = shape
    hidden = blocks * block
    total = SEGS_MAX * ROWS
    last = SEGS_MAX - 1

    def rows(cols):
        return pl.BlockSpec((ROWS, cols), lambda s: (last - s, 0))

    def lanes(height):
        return pl.BlockSpec((height, ROWS), lambda s: (0, last - s))

    def fixed(*shape):
        return pl.BlockSpec(shape, lambda s: (0,) * len(shape))

    seg_block = pl.BlockSpec((1, TEXT, width), lambda s: (last - s, 0, 0))
    sds = jax.ShapeDtypeStruct
    return pl.pallas_call(
        functools.partial(backward_kernel, plan, len(pieces)),
        grid=(SEGS_MAX,),
        in_specs=[scalar(), scalar(), scalar(), seg_block] + [whole()] * 2 + [remain()] * len(pieces)
        + [
            lanes(3 * width), lanes(width), pl.BlockSpec((1, 16, ROWS), lambda s: (last - s, 0, 0)),
            rows(width), rows(1), rows(hidden), rows(width), rows(1),
        ],
        out_specs=[
            rows(width), rows(width), rows(hidden), rows(width), rows(3 * width),
            fixed(8, width), fixed(blocks, block), fixed(MEM, width),
        ],
        out_shape=[
            sds((total, width), f32), sds((total, width), bf16), sds((total, hidden), bf16),
            sds((total, width), bf16), sds((total, 3 * width), bf16),
            sds((8, width), f32), sds((blocks, block), f32), sds((MEM, width), f32),
        ],
        scratch_shapes=[
            pltpu.VMEM((AUG, width), f32), pltpu.VMEM((MEM, width), f32), pltpu.VMEM((ROWS, width), f32),
            pltpu.VMEM((ROWS, width), f32), pltpu.VMEM((ROWS, width), f32),
            pltpu.VMEM((width, ROWS), bf16), pltpu.VMEM((3 * width, ROWS), f32),
        ]
        + weight_scratch(width, blocks, block)
        + [pltpu.SemaphoreType.DMA((3,))],
        compiler_params=pltpu.CompilerParams(vmem_limit_bytes=62 * 2**20),
    )(count, fill, table, out_grad, mem_grad, vec, *pieces, *saved)


class Products:
    def __init__(self, jobs, block, own, small=None, plan=None, n_pieces=0):
        self.jobs, self.block, self.own, self.small, self.plan, self.n_pieces = jobs, block, own, small, plan, n_pieces
        self.loads = []
        for _, loads, _ in jobs:
            self.loads += [load for load in loads if load not in self.loads]

    def part(self, array, load):
        kind = load[1]
        if kind is None:
            return array.shape
        if kind[0] == "rows":
            return (ROWS, array.shape[1])
        return (array.shape[0], self.block)

    def kernel(self, n_in, n_out, index_ref, table_ref, *refs):
        n_loads, n_jobs = len(self.loads), len(self.jobs)
        inputs, refs = refs[:n_in], refs[n_in:]
        pieces, refs = refs[: self.n_pieces], refs[self.n_pieces :]
        outputs, refs = refs[:n_out], refs[n_out:]
        held, refs = refs[:n_loads], refs[n_loads:]
        results, refs = refs[:n_jobs], refs[n_jobs:]
        load_sem, store_sem = refs[:2]
        weights, weight_sem = refs[2:3], refs[3:]
        step = pl.program_id(0)

        def load(n):
            source, kind = self.loads[n]
            view = inputs[source]
            if kind is not None:
                if kind[0] == "rows":
                    view = view.at[pl.ds(kind[1] * ROWS, ROWS), :]
                else:
                    place = index_ref[kind[1]] if kind[0] == "index" else kind[1]
                    view = view.at[:, pl.ds(pl.multiple_of(place * self.block, 128), self.block)]
            return pltpu.make_async_copy(view, held[n], load_sem.at[n])

        needs = [[self.loads.index(x) for x in loads] for _, loads, _ in self.jobs]
        fresh, seen = [], set()
        for need in needs:
            fresh.append([n for n in need if n not in seen])
            seen.update(need)

        def stores(n):
            kind, place, number = self.jobs[n][2]
            result, base = results[n], sum(self.store_counts[:n])
            if kind == "block":
                moves = [(result, outputs[place].at[number])]
            elif kind == "text":
                moves = []
            elif kind == "packed":
                moves = [(result, outputs[place].at[number])]
            else:
                mine, moves = index_ref[0], []
                for j in range(result.shape[0] // 2):
                    moves.append((result.at[2 * j + 1 - mine], outputs[place + 1].at[number, j]))
                    moves.append((result.at[2 * j + mine], outputs[place].at[number, j]))
            return [pltpu.make_async_copy(x, y, store_sem.at[base + m]) for m, (x, y) in enumerate(moves)]

        def shared_rows(n):
            extra = self.small[2]
            ffn = index_ref[self.jobs[n][1][1][1][1]]
            shard = results[n].shape[1] - extra
            return pltpu.make_async_copy(inputs[-1].at[:, ffn], results[n].at[:, pl.ds(shard, extra), :], store_sem.at[sum(self.store_counts) + n])

        for n, (form, _, output) in enumerate(self.jobs):

            @pl.when(step == n)
            def _():
                if n == 0:
                    for m in fresh[0]:
                        load(m).start()
                if output[0] == "packed":
                    shared_rows(n).start()
                for m in fresh[n]:
                    load(m).wait()
                for m in fresh[n + 1] if n + 1 < n_jobs else ():
                    load(m).start()
                texts = [m for m, job in enumerate(self.jobs) if job[0] == "text"]
                if texts and n == texts[0] - 1:
                    start_loads(table_ref, pieces, self.plan, weights, weight_sem[0], (0,))
                if texts and n == texts[0]:
                    wait_loads(weights, weight_sem[0], 0)

            @pl.when(step == n)
            def _():
                if form == "text":
                    seg = output[2]
                    width = weights[0].shape[1]
                    joined = held[needs[n][0]][...]
                    for c in range(3):
                        rows = held[needs[n][1 + c]][seg * ROWS : (seg + 1) * ROWS, :]
                        joined = joined + dot_nt(rows, weights[0][c * width : (c + 1) * width, :])
                    results[n][...] = joined
                    outputs[output[1]][0] = results[n][:TEXT, :]
                else:
                    left, right = needs[n]
                    value = {"tn": dot_tn, "nn": dot_nn}[form](held[left][...], held[right][...]).astype(bf16)
                    if output[0] == "packed":
                        items, rows, _ = results[n].shape
                        shard = rows - self.small[2]
                        results[n][:, :shard, :] = value.reshape(items, shard, self.block)
                        shared_rows(n).wait()
                    else:
                        results[n][...] = value.reshape(results[n].shape)

            @pl.when(step == n)
            def _():
                for copy in stores(n):
                    copy.start()
                if n == n_jobs - 1:
                    for m in range(n_jobs):
                        for copy in stores(m):
                            copy.wait()

    def __call__(self, index, arrays, out_shapes, table=None, pieces=()):
        block, own = self.block, self.own
        width = block
        scratch = [pltpu.VMEM(self.part(arrays[x[0]], x), arrays[x[0]].dtype) for x in self.loads]
        self.store_counts = []
        for form, loads, (kind, _, _) in self.jobs:
            if kind == "text":
                scratch.append(pltpu.VMEM((ROWS, width), f32))
            elif kind == "packed":
                items, _, extra, _ = self.small
                scratch.append(pltpu.VMEM((items, width // items + extra, block), bf16))
            else:
                scratch.append(pltpu.VMEM((width // own, own, block) if kind == "split" else (width, block), bf16))
            self.store_counts.append({"split": width // own, "text": 0}.get(kind, 1))
        scratch += [pltpu.SemaphoreType.DMA((len(self.loads),)), pltpu.SemaphoreType.DMA((sum(self.store_counts) + len(self.jobs),))]
        if pieces:
            scratch += [pltpu.VMEM((4 * width, width), bf16), pltpu.SemaphoreType.DMA((1,))]
        ahead = len(self.jobs) - SEGS_MAX
        text_block = pl.BlockSpec((1, TEXT, width), lambda j: (jnp.maximum(j - ahead, 0), 0, 0))
        return pl.pallas_call(
            functools.partial(self.kernel, len(arrays), len(out_shapes)),
            grid=(len(self.jobs),),
            in_specs=[scalar(), scalar()] + [remain()] * (len(arrays) + len(pieces)),
            out_specs=[remain() if dtype == bf16 else text_block for _, dtype in out_shapes],
            out_shape=[jax.ShapeDtypeStruct(shape, dtype) for shape, dtype in out_shapes],
            scratch_shapes=scratch,
            compiler_params=pltpu.CompilerParams(vmem_limit_bytes=62 * 2**20),
        )(index, index if table is None else table, *arrays, *pieces)


def text_grad_kernel(plan, n_pieces, table_ref, first_ref, gqkv_ref, *refs):
    pieces = refs[:n_pieces]
    out_ref, joined_ref, attn_ref, sems = refs[n_pieces:]
    width = attn_ref.shape[1]

    @pl.when(pl.program_id(0) == 0)
    def _():
        start_loads(table_ref, pieces, plan, (attn_ref,), sems, (0,))
        wait_loads((attn_ref,), sems, 0)

    joined = first_ref[...]
    for c in range(3):
        joined = joined + dot_nt(gqkv_ref[:, c * width : (c + 1) * width], attn_ref[c * width : (c + 1) * width, :])
    joined_ref[...] = joined
    out_ref[0] = joined_ref[:TEXT, :]


def text_grad_call(first, gqkv, table, plan, pieces):
    width = first.shape[1]

    def rows(cols):
        return pl.BlockSpec((ROWS, cols), lambda s: (s, 0))

    return pl.pallas_call(
        functools.partial(text_grad_kernel, plan, len(pieces)),
        grid=(SEGS_MAX,),
        in_specs=[scalar(), rows(width), rows(3 * width)] + [remain()] * len(pieces),
        out_specs=pl.BlockSpec((1, TEXT, width), lambda s: (s, 0, 0)),
        out_shape=jax.ShapeDtypeStruct((SEGS_MAX, TEXT, width), f32),
        scratch_shapes=[
            pltpu.VMEM((ROWS, width), f32), pltpu.VMEM((4 * width, width), bf16), pltpu.SemaphoreType.DMA((1,)),
        ],
        compiler_params=pltpu.CompilerParams(vmem_limit_bytes=62 * 2**20),
    )(table, first, gqkv, *pieces)


def deal_kernel(outputs, places, n_in, n_out, index_ref, *refs):
    inputs, refs = refs[:n_in], refs[n_in:]
    outs, refs = refs[:n_out], refs[n_out:]
    load_sem, store_sem = refs[-2:]
    held = list(refs[:-2])
    results = held[-len(outputs) :]

    def view(array, indices):
        found = []
        for index in indices:
            if index is None:
                found.append(slice(None))
            elif isinstance(index, int):
                found.append(index)
            elif index[0] == "at":
                found.append(index_ref[index[1]] + index[2])
            else:
                found.append(pl.ds(index[0], index[1] - index[0]))
        return inputs[array].at[tuple(found)]

    waits, number = [], 0
    for _, views in outputs:
        waits.append([])
        for item in views:
            target, sem = held[number], load_sem.at[number]
            number += 1
            one = pltpu.make_async_copy(view(*item[:2]), target, sem)
            if len(item) == 2:
                one.start()
            else:
                (other, which) = item[2:]
                two = pltpu.make_async_copy(view(*other), target, sem)
                pl.when(index_ref[which] == 0)(one.start)
                pl.when(index_ref[which] != 0)(two.start)
            waits[-1].append((one, target))
    stores = []
    for n, items in enumerate(waits):
        total = None
        for copy, target in items:
            copy.wait()
            part = target[...].astype(f32)
            total = part if total is None else total + part
        results[n][...] = total.astype(bf16)
        out, first = places[n]
        target = outs[out] if first is None else outs[out].at[pl.ds(first, results[n].shape[0]), :]
        stores.append(pltpu.make_async_copy(results[n], target, store_sem.at[n]))
        stores[-1].start()
    for copy in stores:
        copy.wait()


def deal(index, outputs):
    arrays, places, shapes, flat = [], [], [], []
    for n, output in enumerate(outputs):
        if isinstance(output, list):
            first = 0
            for part in output:
                places.append((n, first))
                first += part[0][0]
                flat.append(part)
            shapes.append((first,) + output[0][0][1:])
        else:
            places.append((n, None))
            flat.append(output)
            shapes.append(output[0])
    outputs = flat

    def place(array):
        for n, known in enumerate(arrays):
            if known is array:
                return n
        arrays.append(array)
        return len(arrays) - 1

    plain = []
    for shape, views in outputs:
        plain.append((shape, [
            (place(v[0]), v[1]) if len(v) == 2 else (place(v[0]), v[1], (place(v[2][0]), v[2][1]), v[3]) for v in views
        ]))
    scratch = [pltpu.VMEM(shape, bf16) for shape, views in plain for _ in views]
    n_loads = len(scratch)
    scratch += [pltpu.VMEM(shape, bf16) for shape, _ in plain]
    scratch += [pltpu.SemaphoreType.DMA((n_loads,)), pltpu.SemaphoreType.DMA((len(plain),))]
    return pl.pallas_call(
        functools.partial(deal_kernel, plain, places, len(arrays), len(shapes)),
        in_specs=[scalar()] + [remain()] * len(arrays),
        out_specs=[remain()] * len(shapes),
        out_shape=[jax.ShapeDtypeStruct(shape, bf16) for shape in shapes],
        scratch_shapes=scratch,
        compiler_params=pltpu.CompilerParams(vmem_limit_bytes=62 * 2**20),
    )(index, *arrays)


class Piece:
    MINE = {"t": 4, "y": 6}

    def __init__(self, halves):
        self.halves = halves
        self.shard = halves[0][0][0].shape[-2:]

    def views(self, half, chosen):
        out = []
        for array, names, first in self.halves[half]:
            at = []
            for name in names:
                if name in chosen:
                    at.append(chosen[name])
                elif name == "s":
                    at.append((first, first + 2))
                else:
                    at.append(None)
            out.append((array, tuple(at)))
        return out

    def plane(self, step):
        outputs, self.names = [], []
        for half, order in enumerate(PLANE):
            axis = order[step][0]
            chosen = {axis: ("at", self.MINE[axis] + 1, 0)}
            if step == 1:
                chosen[order[0][0]] = ("at", self.MINE[order[0][0]], 0)
            names = [n for n in self.halves[half][0][1] if n not in chosen]
            outputs.append((tuple(2 for _ in names) + self.shard, self.views(half, chosen)))
            self.names.append(names)
        return outputs

    def swap_plane(self, step, sends):
        self.arrived = [swap(x, order[step][0], 2, 1) for x, order in zip(sends, PLANE)]

    def take(self):
        for half, (value, names) in enumerate(zip(self.arrived, self.names)):
            self.halves[half] = self.halves[half] + [(value, names, 0)]

    def line(self):
        outputs = []
        for mask in range(4):
            views = []
            here = {"t": ("at", 4, 0), "y": ("at", 6, 0)}
            for (a, names, first), (b, other_names, other_first) in zip(*self.halves):
                def at(names, first):
                    return tuple(("at", 12 + mask, first) if n == "s" else here[n] for n in names)
                views.append((a, at(names, first), (b, at(other_names, other_first)), 8 + mask))
            outputs.append((self.shard, views))
        return outputs

    def total(self, kept, arrived):
        return sum(x.astype(f32) for x in [kept] + arrived)


def swap(value, axis, size, mask):
    return lax.ppermute(value, axis, [(i, i ^ mask) for i in range(size)])


def after(value, *others):
    return lax.optimization_barrier((value, others))[0]


def moved(coords, place, mask):
    return [c[:place] + (c[place] ^ mask,) + c[place + 1 :] for c in coords]


PLANE = ((("t", 1), ("y", 2)), (("y", 2), ("t", 1)))


def gather_line(shard, sizes, beside):
    parts = [swap(shard, "s", sizes["s"], m) for m in range(1, sizes["s"])]
    parts, beside = lax.optimization_barrier((parts, beside))
    parts = [shard] + parts
    half = sizes["s"] // 2
    return (jnp.concatenate(parts[:half]), jnp.concatenate(parts[half:])), beside


def gather_first(halves, sizes, beside):
    arrived = []
    for value, ((axis, _), _) in zip(halves, PLANE):
        arrived.append([swap(value, axis, sizes[axis], m) for m in range(1, sizes[axis])])
    arrived, beside = lax.optimization_barrier((arrived, beside))
    return tuple(jnp.concatenate([value] + more) for value, more in zip(halves, arrived)), beside


def gather_last(values, sizes):
    return tuple(
        tuple(swap(value, axis, sizes[axis], m) for m in range(1, sizes[axis]))
        for value, (_, (axis, _)) in zip(values, PLANE)
    )


def gather_core(first, last, sizes):
    out = []
    half = sizes["s"] // 2
    for number, (value, more, ((axis, place), (last_axis, last_place))) in enumerate(zip(first, last, PLANE)):
        coords = [(m, 0, 0, 0) for m in range(number * half, (number + 1) * half)]
        coords = sum((moved(coords, place, m) for m in range(sizes[axis])), [])
        out.append((value, coords))
        out += [(extra, moved(coords, last_place, m)) for m, extra in enumerate(more, 1)]
    return out + [
        (swap(value, "c", sizes["c"], m), moved(coords, 3, m))
        for m in range(1, sizes["c"])
        for value, coords in out
    ]


def pick(value, axis, index):
    return lax.dynamic_index_in_dim(value, index, axis, keepdims=False)


def body(sizes, text_rows, attn_weight, vectors, w_in, b_in, w_out, seg_count, last_fill, out_grad, mem_grad):
    width = text_rows.shape[-1]
    block = w_in.shape[1]
    n_s, n_t, n_y, n_c = (sizes[a] for a in "styc")
    n_ffn, n_items = n_y * n_c, n_s * n_t
    devices = n_ffn * n_items
    shard = width // n_items
    own = attn_weight.shape[0]
    me = {a: lax.axis_index(a) for a in "styc"}

    small = jnp.concatenate([vectors.reshape(-1), b_in.reshape(-1)])
    vec_size, small_size = vectors.size, small.size
    small_rows = -(-small_size // (width * 16)) * 16
    small = jnp.pad(small, (0, small_rows * width - small_size)).reshape(small_rows, width)
    direct = own % 16 == 0 and shard % 16 == 0 and (n_s, n_t, n_y, n_c) == (4, 2, 2, 2)

    def absolute(masks):
        return [me[a] ^ m for a, m in zip("styc", masks)]

    if direct:
        text = with_layout_constraint(text_rows[0], Layout((0, 1, 2)))
        grads = with_layout_constraint(out_grad[0], Layout((0, 1, 2)))
        line, text = gather_line(jnp.concatenate([attn_weight, small]), sizes, text)
        first, grads = gather_first(line, sizes, grads)
        text_rows, out_grad = text[None], grads[None]
        last = gather_last(first, sizes)
        feeds = lax.all_gather(jnp.concatenate([w_in, w_out.T]), ("s", "t", "y", "c"), axis=0, tiled=True)
        gathered = [gather_core(first, last, sizes)]
        plan, table, pieces, smalls = [], [], [], []
        for target, found in enumerate(gathered):
            for value, coords in found:
                each = value.shape[0] // len(coords)
                for j, masks in enumerate(coords):
                    s, t, y, c = absolute(masks)
                    item, ffn = s * n_t + t, y * n_c + c
                    if target == 0:
                        plan.append((len(pieces), j * each, own, 0))
                        table.append((item * n_ffn + ffn) * own)
                        smalls.append((item * n_ffn + ffn, value[j * each + own]))
                    else:
                        plan.append((len(pieces), j * each, shard, target))
                        table.append(ffn * width + item * shard)
                pieces.append(value)
        for device in range(devices):
            item, ffn = device // n_ffn, device % n_ffn
            for target in (1, 2):
                plan.append((len(pieces), (2 * device + target - 1) * shard, shard, target))
                table.append(jnp.int32(ffn * width + item * shard))
        pieces.append(feeds)
        place = jnp.stack([d for d, _ in smalls])
        rows = jnp.stack([row for _, row in smalls])
        rows = rows[jnp.argsort(place)][:, :small_size]
    else:
        def all_of(value):
            return lax.all_gather(value, ("s", "t", "y", "c"), axis=0)

        def by_block(value):
            parts = all_of(value).reshape(n_items, n_ffn, shard, block)
            return parts.transpose(1, 0, 2, 3).reshape(n_ffn * width, block)

        pieces = [all_of(attn_weight).reshape(-1, width), by_block(w_in), by_block(w_out.T)]
        plan = [(i, 0, p.shape[0], i) for i, p in enumerate(pieces)]
        table = [jnp.int32(0)] * 3
        rows = all_of(small).reshape(devices, -1)[:, :small_size]
    table = jnp.stack(table).astype(jnp.int32)
    rows = rows.astype(f32)
    vec = rows[:, :vec_size].reshape(devices, vectors.shape[0], -1).transpose(1, 0, 2).reshape(-1, width)
    bias = rows[:, vec_size:].reshape(n_items, n_ffn, -1).transpose(1, 0, 2).reshape(n_ffn, block)
    col = vec[:2].T

    attn_plan = [entry for entry in plan if entry[3] == 0]
    attn_used = sorted({entry[0] for entry in attn_plan})
    attn_plan = [(attn_used.index(entry[0]),) + entry[1:] for entry in attn_plan]
    attn_pieces = [pieces[n] for n in attn_used]
    early = early_call(seg_count, last_fill, text_rows[0], col, table, attn_plan, attn_pieces)

    (activations, memory, zl, qkv, mixed, lse, n1, r1, hl, act, slope, n2, r2) = forward_call(
        seg_count, last_fill, text_rows[0], bias, vec, early, table, plan, pieces
    )
    first_grad, gbranch, gpre, gattn, gqkv, vgrad, bgrad, gmem = backward_call(
        seg_count, last_fill, out_grad[0], mem_grad, vec,
        (qkv, mixed, lse, n1, r1, slope, n2, r2), (n_ffn, block), table, plan, pieces,
    )

    n_vec = vectors.shape[0]

    small_total = jnp.concatenate([vgrad, gmem])

    if direct:
        mine = me["c"].astype(jnp.int32)
        index = jnp.stack([mine] + [n_c * y + mine for y in range(n_y)] + [n_c * y + 1 - mine for y in range(n_y)])

        def blocks_of(left, right, which, output, kind="block"):
            return [
                ("tn", ((left, None), (right, ("index", 1 + which * n_y + y))), (kind, output, y)) for y in range(n_y)
            ]

        plain = ((n_y, width, block), bf16)
        packed = ((n_y, n_items, shard + 16, block), bf16)
        dealt = [((4, width // own // 2, own, width), bf16)] * 2

        (out_send,) = Products(blocks_of(0, 1, 1, 0), block, own)(index, (gbranch, act), [plain])
        out_arrived = swap(out_send, "c", n_c, 1)
        small = jnp.concatenate(
            [
                small_total.reshape(n_vec, devices, -1).transpose(1, 0, 2).reshape(devices, -1),
                bgrad.reshape(n_ffn, n_items, -1).transpose(1, 0, 2).reshape(devices, -1),
            ],
            axis=1,
        ).astype(bf16)
        small = jnp.pad(small, ((0, 0), (0, 16 * block - small_size))).reshape(n_items, n_ffn, 16, block)
        out_keep, in_send = Products(
            blocks_of(0, 1, 0, 0) + blocks_of(2, 3, 1, 1, "packed"), block, own, small.shape
        )(index, (after(gbranch, out_send), act, hl, gpre, small), [plain, packed])

        def shaped(value):
            return value.reshape(n_y, n_s, n_t, -1, block)

        def attn_shaped(value):
            return value.reshape(n_s, n_t, n_y, own, width)

        out_arrived, out_keep, in_send = lax.optimization_barrier((out_arrived, out_keep, in_send))
        lines = [me["s"] ^ m for m in range(4)]
        grid_index = jnp.stack(
            lines + [me["t"], me["t"] ^ 1, me["y"], me["y"] ^ 1] + [x // 2 for x in lines] + [x % 2 for x in lines]
        ).astype(jnp.int32)

        def deal_all(*groups):
            found, out = deal(grid_index, sum(groups, [])), []
            for group in groups:
                out.append(found[: len(group)])
                found = found[len(group) :]
            return out

        out = Piece([[(shaped(x), "yst", 2 * n) for x in (out_keep, out_arrived)] for n in range(2)])
        (sends,) = deal_all(out.plane(0))
        out.swap_plane(0, sends)
        in_arrived = swap(in_send, "c", n_c, 1)
        in_keep, attn_keep, attn_send = Products(
            blocks_of(0, 1, 0, 0, "packed")
            + [("tn", ((2, None), (3, ("column", c))), ("split", 1, c)) for c in range(3)]
            + [("nn", ((4, None), (5, None)), ("split", 1, 3))],
            block, own, small.shape,
        )(index, (after(hl, sends), gpre, zl, gqkv, mixed, gattn, small), [packed] + dealt)
        out.arrived, in_arrived, in_keep, attn_keep, attn_send = lax.optimization_barrier(
            (out.arrived, in_arrived, in_keep, attn_keep, attn_send)
        )

        out.take()
        feed = Piece([[(shaped(x), "yst", 2 * n) for x in (in_keep, in_arrived)] for n in range(2)])
        sends, more = deal_all(out.plane(1), feed.plane(0))
        out.swap_plane(1, sends)
        feed.swap_plane(0, more)
        attn_arrived = swap(attn_send, "c", n_c, 1)
        text_grad = text_grad_call(after(first_grad, sends, more), gqkv, table, attn_plan, attn_pieces)
        out.arrived, feed.arrived, attn_arrived, text_grad = lax.optimization_barrier(
            (out.arrived, feed.arrived, attn_arrived, text_grad)
        )

        out.take()
        feed.take()
        last = Piece([[(attn_shaped(x), "sty", 2 * n) for x in (attn_keep, attn_arrived)] for n in range(2)])
        out_line = out.line()
        more, lasts, (out_kept, out_two) = deal_all(feed.plane(1), last.plane(0), [out_line[0], out_line[2]])
        last.swap_plane(0, lasts)
        feed.swap_plane(1, more)
        out_two = swap(out_two, "s", 4, 2)
        text_grad = with_layout_constraint(after(text_grad, more).transpose(1, 0, 2), Layout((0, 1, 2)))
        out_two, feed.arrived, last.arrived, text_grad = lax.optimization_barrier(
            (out_two, feed.arrived, last.arrived, text_grad)
        )

        feed.take()
        last.take()
        in_line = feed.line()
        more, (in_kept, in_two, one, three) = deal_all(
            last.plane(1), [in_line[0], in_line[2], [out_line[1], in_line[1]], [out_line[3], in_line[3]]]
        )
        last.swap_plane(1, more)
        one, three, in_two = swap(one, "s", 4, 1), swap(three, "s", 4, 3), swap(in_two, "s", 4, 2)
        activations = with_layout_constraint(after(activations, more).transpose(1, 0, 2), Layout((0, 1, 2)))
        one, three, in_two, last.arrived, activations = lax.optimization_barrier(
            (one, three, in_two, last.arrived, activations)
        )

        last.take()
        attn_kept, *lines = deal_all(last.line())[0]
        lines = [swap(part, "s", 4, m) for m, part in enumerate(lines, 1)]
        w_out_grad = out.total(out_kept, [one[:shard], out_two, three[:shard]]).T
        in_own = feed.total(in_kept, [one[shard:], in_two, three[shard:]])
        w_in_grad = in_own[:shard]
        small_own = in_own[shard:].reshape(-1)[:small_size]
        vector_grad = small_own[:vec_size].reshape(vectors.shape)
        b_in_grad = small_own[vec_size:].reshape(b_in.shape)
        attn_grad = last.total(attn_kept, lines)
        activations, text_grad = activations.transpose(1, 0, 2), text_grad.transpose(1, 0, 2)
    else:
        axes = ("s", "t", "y", "c")

        def scatter_block(left, right):
            total = dot_tn(left, right).astype(bf16).reshape(n_items, shard, n_ffn, block).transpose(0, 2, 1, 3)
            total = total.reshape(devices, shard, block)
            return lax.psum_scatter(total, axes, scatter_dimension=0, tiled=False).astype(f32)

        w_out_grad = scatter_block(gbranch, act).T
        w_in_grad = scatter_block(hl, gpre)
        total = [dot_tn(zl, gqkv[:, c * width : (c + 1) * width]) for c in range(3)] + [dot_nn(mixed, gattn)]
        total = jnp.concatenate(total).astype(bf16)
        attn_grad = lax.psum_scatter(total, axes, scatter_dimension=0, tiled=True).astype(f32)
        vector_grad = lax.psum_scatter(small_total, axes, scatter_dimension=1, tiled=True)
        b_total = bgrad.reshape(n_ffn, n_items, -1).transpose(1, 0, 2).reshape(devices, 1, -1)
        b_in_grad = lax.psum_scatter(b_total, axes, scatter_dimension=0, tiled=False)
        text_grad = text_grad_call(first_grad, gqkv, table, attn_plan, attn_pieces)
    return (activations[None], memory[None], text_grad[None], attn_grad, vector_grad, w_in_grad, b_in_grad, w_out_grad)


def solution(mesh):
    items, ffn = mesh.shape["items"], mesh.shape["ffn"]
    sizes = {"s": 4, "t": items // 4, "y": ffn // 2, "c": 2}
    grid = jax.sharding.Mesh(mesh.devices.reshape(tuple(sizes.values())), tuple(sizes))
    both, item, feed = P(("s", "t", "y", "c")), ("s", "t"), ("y", "c")
    last = P(None, ("s", "t", "y", "c"))
    return jax.shard_map(
        functools.partial(body, sizes),
        mesh=grid,
        in_specs=(both, both, last, P(item, feed), P(feed, item), P(feed, item), both, both, both, both),
        out_specs=(both, both, both, both, last, P(item, feed), P(feed, item), P(feed, item)),
        check_vma=False,
    )
```

profile of v0, /device:TPU:0, one launch (start us, length us, event | category | flops | bytes accessed | tf_op | source)
XLA Modules:
  0.0 399.7 jit_solution(12438442584881664136)
XLA Ops:
  7.2 1.7 pad_maximum_fusion.2
  10.5 0.9 constant_dynamic-update-slice_fusion.5
  11.5 5.1 %collective-permute-start.2 = (bf16[112,768]{1,0:T(8,128)(2,1)S(1)}, bf16[112,768]{1,0:T(8,128)(2,1)S(1)}, u32[]{:S(2)}, u32[]{:S(2)}) collective-permute-start(bf16[112,768]{1,0:T(8,128)(2,1)S(1)} %get-tuple-element.253), channel_id=1, source_target_pairs={{0,24},{8,16},{16,8},{24,0},{1,25},{9,17},{17,9},{25,1},{2,26},{10... | collective-permute-start | bytes 516104 | tf_op jit(solution)/shard_map/ppermute | solution.py:880
  17.2 4.0 %copy.77 = bf16[1,4,502,768]{3,2,1,0:T(8,128)(2,1)} copy(bf16[1,4,502,768]{3,1,2,0:T(4,128)(2,1)} %param.10) | data formatting | bytes 6168576 | tf_op args[0]
  21.3 2.0 copy.76
  23.4 1.6 sort.17
  25.0 12.4 %collective-permute-done.1 = bf16[112,768]{1,0:T(8,128)(2,1)S(1)} collective-permute-done((bf16[112,768]{1,0:T(8,128)(2,1)S(1)}, bf16[112,768]{1,0:T(8,128)(2,1)S(1)}, u32[]{:S(2)}, u32[]{:S(2)}) %collective-permute-start.1) | collective-permute-done | bytes 172064 | tf_op jit(solution)/shard_map/ppermute | solution.py:880
  37.4 1.6 collective-permute-start.4
  39.1 1.6 collective-permute-start.3
  40.7 9.7 %collective-permute-done.4 = bf16[224,768]{1,0:T(8,128)(2,1)S(1)} collective-permute-done((bf16[224,768]{1,0:T(8,128)(2,1)S(1)}, bf16[224,768]{1,0:T(8,128)(2,1)S(1)}, u32[]{:S(2)}, u32[]{:S(2)}) %collective-permute-start.4) | collective-permute-done | bytes 344096 | tf_op jit(solution)/shard_map/ppermute | solution.py:880
  50.4 4.4 %collective-permute-done.3 = bf16[224,768]{1,0:T(8,128)(2,1)S(1)} collective-permute-done((bf16[224,768]{1,0:T(8,128)(2,1)S(1)}, bf16[224,768]{1,0:T(8,128)(2,1)S(1)}, u32[]{:S(2)}, u32[]{:S(2)}) %collective-permute-start.3) | collective-permute-done | bytes 344096 | tf_op jit(solution)/shard_map/ppermute | solution.py:880
  55.5 2.5 collective-permute-start.6
  63.0 2.8 collective-permute-done.5.refs_1_.refs_4_
  65.8 4.4 %collective-permute-done.6.refs_3_.refs_6_ = bf16[448,768]{1,0:T(8,128)(2,1)S(1)} collective-permute-done((bf16[448,768]{1,0:T(8,128)(2,1)S(1)}, bf16[448,768]{1,0:T(8,128)(2,1)S(1)}, u32[]{:S(2)}, u32[]{:S(2)}) %collective-permute-start.6) | collective-permute-done | bytes 688160 | tf_op jit(solution)/shard_map/ppermute | solution.py:880
  70.2 0.9 fusion.9
  71.3 1.1 collective-permute-done.10.refs_7_.refs_10_
  76.0 1.0 copy.61
  76.9 29.5 %shard_map.161 = (bf16[2304,2048]{1,0:T(8,128)(2,1)}, bf16[768,2048]{1,0:T(8,128)(2,1)}, f32[4,16,512]{2,1,0:T(8,128)}) custom-call(s32[1]{0:T(128)S(6)} %copy.86.count_ref, s32[1]{0:T(128)S(6)} %copy.87.fill_ref, s32[96]{0:T(128)} %stack.322.table_ref, bf16[4,502,768]{2,1,0:T(8,128)(2,1)} %bitcast.153, f32[768,2]{1,0:T(8,128)} %bitcast.161, ...), custom_call_target="tpu_custom_call" | custom-call | tf_op jit(solution)/shard_map/pallas_call | solution.py:173
  106.5 51.1 %shard_map.162 = (bf16[4,502,768]{2,1,0:T(8,128)(2,1)}, f32[10,768]{1,0:T(8,128)}, bf16[2048,768]{1,0:T(8,128)(2,1)}, bf16[2304,2048]{1,0:T(8,128)(2,1)}, bf16[7...) custom-call(s32[1]{0:T(128)S(6)} %copy.86.count_ref, ...), custom_call_target="tpu_custom_call" | custom-call | tf_op jit(solution)/shard_map/pallas_call | solution.py:473
  157.5 73.2 %shard_map.163 = (f32[2048,768]{1,0:T(8,128)}, bf16[2048,768]{1,0:T(8,128)(2,1)}, bf16[2048,3072]{1,0:T(8,128)(2,1)}, bf16[2048,768]{1,0:T(8,128)(2,1)}, bf16[20...) custom-call(s32[1]{0:T(128)S(6)} %copy.86.count_ref, s32[1]{0:T(128)S(6)} %copy.87.fill_ref, ...), custom_call_target="tpu_custom_call" | custom-call | tf_op jit(solution)/shard_map/pallas_call | solution.py:521
  230.8 10.1 %shard_map.164 = bf16[2,768,768]{2,1,0:T(8,128)(2,1)} custom-call(s32[5]{0:T(128)} %stack.289.index_ref.table_ref, s32[5]{0:T(128)} %stack.289.index_ref.table_ref, bf16[2048,768]{1,0:T(8,128)(2,1)} %get-tuple-element.120.refs_0_, bf16[2048,3072]{1,0:T(8,128)(2,1)} %get-tuple-element.119.refs_1_), custom_call_target="tpu_custom_call" | custom-call | tf_op jit(solution)/shard_map/pallas_call | solution.py:683
  241.8 1.0 copy.69
  242.8 16.2 %shard_map.165 = (bf16[2,768,768]{2,1,0:T(8,128)(2,1)}, bf16[2,8,112,768]{3,2,1,0:T(8,128)(2,1)}) custom-call(s32[5]{0:T(128)} %stack.289.index_ref.table_ref, s32[5]{0:T(128)} %stack.289.index_ref.table_ref, bf16[2048,768]{1,0:T(8,128)(2,1)} %get-tuple-element.120.refs_0_, bf16[2048,3072]{1,0:T(8,128)(2,1)} %get-tuple-element.119.refs_1_, ...), custom_call_target="tpu_custom_call" | custom-call | tf_op jit(solution)/shard_map/pallas_call | solution.py:683
  259.8 3.2 shard_map.166
  263.1 1.7 collective-permute-start.12
  265.1 22.8 %shard_map.167 = (bf16[2,8,112,768]{3,2,1,0:T(8,128)(2,1)}, bf16[4,4,96,768]{3,2,1,0:T(8,128)(2,1)}, bf16[4,4,96,768]{3,2,1,0:T(8,128)(2,1)}) custom-call(s32[5]{0:T(128)} %stack.289.index_ref.table_ref, s32[5]{0:T(128)} %stack.289.index_ref.table_ref, bf16[2048,768]{1,0:T(8,128)(2,1)} %get-tuple-element.133.refs_2_.refs_0_, ...), custom_call_target="tpu_custom_call" | custom-call | tf_op jit(solution)/shard_map/pallas_call | solution.py:683
  289.1 4.1 %shard_map.168 = (bf16[2,96,768]{2,1,0:T(8,128)(2,1)}, bf16[2,96,768]{2,1,0:T(8,128)(2,1)}, bf16[2,2,112,768]{3,2,1,0:T(8,128)(2,1)}, bf16[2,2,112,768]{3,2,1,0:T(8,128)(2,1)}) custom-call(s32[16]{0:T(128)} %stack.284.index_ref, bf16[2,4,2,96,768]{4,3,2,1,0:T(8,128)(2,1)} %bitcast.135, ...), custom_call_target="tpu_custom_call" | custom-call | tf_op jit(solution)/shard_map/pallas_call | solution.py:813
  293.2 0.9 collective-permute-start.17
  294.1 1.2 collective-permute-start.18
  296.2 1.2 collective-permute-start.16
  297.3 15.0 %shard_map.169 = f32[4,502,768]{2,1,0:T(8,128)} custom-call(s32[96]{0:T(128)} %stack.322.table_ref, f32[2048,768]{1,0:T(8,128)} %get-tuple-element.151.first_ref, bf16[2048,2304]{1,0:T(8,128)(2,1)} %get-tuple-element.135.refs_3_.gqkv_ref, bf16[448,768]{1,0:T(8,128)(2,1)} %copy-done.1, bf16[448,768]{1,0:T(8,128)(2,1)} %copy-done.2, bf16[448,768]{1,0:T(8,128)(2,1)} %copy-done, ...), custom_call_target="tpu_custom_call" | custom-call | tf_op jit(solution)/shard_map/pallas_call | solution.py:717
  312.3 5.2 %collective-permute-done.15.refs_16_.refs_20_ = bf16[2,96,768]{2,1,0:T(8,128)(2,1)S(1)} collective-permute-done((bf16[2,96,768]{2,1,0:T(8,128)(2,1)}, bf16[2,96,768]{2,1,0:T(8,128)(2,1)S(1)}, u32[]{:S(2)}, u32[]{:S(2)}) %collective-permute-start.15) | collective-permute-done | bytes 294944 | tf_op jit(solution)/shard_map/ppermute | solution.py:880
  318.8 4.4 %shard_map.170 = (bf16[2,112,768]{2,1,0:T(8,128)(2,1)}, bf16[2,112,768]{2,1,0:T(8,128)(2,1)}, bf16[2,2,96,768]{3,2,1,0:T(8,128)(2,1)}, bf16[2,2,96,768]{3,2,1,0:...) custom-call(s32[16]{0:T(128)} %stack.284.index_ref, bf16[2,4,2,112,768]{4,3,2,1,0:T(8,128)(2,1)} %bitcast.143, ...), custom_call_target="tpu_custom_call" | custom-call | tf_op jit(solution)/shard_map/pallas_call | solution.py:813
  323.2 1.2 collective-permute-start.23
  324.4 1.6 collective-permute-start.24
  327.7 7.8 %copy.75 = f32[4,502,768]{2,0,1:T(4,128)} copy(f32[4,502,768]{2,1,0:T(8,128)} %shard_map.169) | data formatting | bytes 12337152 | tf_op jit(solution)/shard_map/optimization_barrier | solution.py:884
  335.5 10.0 %collective-permute-done.21.refs_12_ = bf16[2,112,768]{2,1,0:T(8,128)(2,1)S(1)} collective-permute-done((bf16[2,112,768]{2,1,0:T(8,128)(2,1)}, bf16[2,112,768]{2,1,0:T(8,128)(2,1)S(1)}, u32[]{:S(2)}, u32[]{:S(2)}) %collective-permute-start.21) | collective-permute-done | bytes 344096 | tf_op jit(solution)/shard_map/ppermute | solution.py:880
  346.8 4.8 %shard_map.171 = (bf16[2,96,768]{2,1,0:T(8,128)(2,1)}, bf16[2,96,768]{2,1,0:T(8,128)(2,1)}, bf16[112,768]{1,0:T(8,128)(2,1)}, bf16[112,768]{1,0:T(8,128)(2,1)}, ...) custom-call(s32[16]{0:T(128)} %stack.284.index_ref, bf16[4,2,2,96,768]{4,3,2,1,0:T(8,128)(2,1)} %bitcast.149, ...), custom_call_target="tpu_custom_call" | custom-call | tf_op jit(solution)/shard_map/pallas_call | solution.py:813
  351.7 2.9 collective-permute-start.26
  354.6 1.7 collective-permute-start.28
  357.9 4.7 %copy.78 = bf16[4,502,768]{2,0,1:T(4,128)(2,1)} copy(bf16[4,502,768]{2,1,0:T(8,128)(2,1)} %get-tuple-element.174) | data formatting | bytes 6168576 | tf_op jit(solution)/shard_map/optimization_barrier | solution.py:884
  362.7 11.7 %collective-permute-done.27 = bf16[112,768]{1,0:T(8,128)(2,1)S(1)} collective-permute-done((bf16[112,768]{1,0:T(8,128)(2,1)}, bf16[112,768]{1,0:T(8,128)(2,1)S(1)}, u32[]{:S(2)}, u32[]{:S(2)}) %collective-permute-start.27) | collective-permute-done | bytes 172064 | tf_op jit(solution)/shard_map/ppermute | solution.py:880
  375.5 3.4 shard_map.172
  378.9 3.2 collective-permute-start.31
  382.1 1.2 collective-permute-start.32
  385.3 1.4 collective-permute-done.30
  386.6 4.3 %collective-permute-done.31 = bf16[96,768]{1,0:T(8,128)(2,1)S(1)} collective-permute-done((bf16[96,768]{1,0:T(8,128)(2,1)}, bf16[96,768]{1,0:T(8,128)(2,1)S(1)}, u32[]{:S(2)}, u32[]{:S(2)}) %collective-permute-start.31) | collective-permute-done | bytes 147488 | tf_op jit(solution)/shard_map/ppermute | solution.py:880
  391.0 1.7 convert_add_fusion.1
  (200 shorter events, 23.2 us)
Async XLA Ops:
  7.2 99.3 %all-gather.2.cloned.1.call-start = ((), (), s32[]{:S(2)}) async-start(), calls=%async_computation | async-start | bytes 9732096 | tf_op jit(solution)/shard_map/all_gather | solution.py:962
  11.5 13.6 %collective-permute-start.2 = (bf16[112,768]{1,0:T(8,128)(2,1)S(1)}, bf16[112,768]{1,0:T(8,128)(2,1)S(1)}, u32[]{:S(2)}, u32[]{:S(2)}) collective-permute-start(bf16[112,768]{1,0:T(8,128)(2,1)S(1)} %get-tuple-element.253), channel_id=1, source_target_pairs={{0,24},{8,16},{16,8},{24,0},{1,25},{9,17},{17,9},{25,1},{2,26},{10... | collective-permute-start | bytes 516104 | tf_op jit(solution)/shard_map/ppermute | solution.py:880
  16.6 20.8 %collective-permute-start.1 = (bf16[112,768]{1,0:T(8,128)(2,1)S(1)}, bf16[112,768]{1,0:T(8,128)(2,1)S(1)}, u32[]{:S(2)}, u32[]{:S(2)}) collective-permute-start(bf16[112,768]{1,0:T(8,128)(2,1)S(1)} %get-tuple-element.253), channel_id=1, source_target_pairs={{0,16},{8,24},{16,0},{24,8},{1,17},{9,25},{17,1},{25,9},{2,18},{10... | collective-permute-start | bytes 516104 | tf_op jit(solution)/shard_map/ppermute | solution.py:880
  16.6 20.8 %collective-permute-start = (bf16[112,768]{1,0:T(8,128)(2,1)S(1)}, bf16[112,768]{1,0:T(8,128)(2,1)S(1)}, u32[]{:S(2)}, u32[]{:S(2)}) collective-permute-start(bf16[112,768]{1,0:T(8,128)(2,1)S(1)} %get-tuple-element.253), channel_id=1, source_target_pairs={{0,8},{8,0},{16,24},{24,16},{1,9},{9,1},{17,25},{25,17},{2,10},{10... | collective-permute-start | bytes 516104 | tf_op jit(solution)/shard_map/ppermute | solution.py:880
  21.3 17.7 %copy-start.16 = (bf16[96,768]{1,0:T(8,128)(2,1)S(1)}, bf16[96,768]{1,0:T(8,128)(2,1)}, u32[]{:S(2)}) copy-start(bf16[96,768]{1,0:T(8,128)(2,1)} %param.11) | copy-start | bytes 442372
  23.3 36.1 %copy-start.29 = (f32[1,10,768]{2,0,1:T(1,128)S(1)}, f32[1,10,768]{2,0,1:T(1,128)}, u32[]{:S(2)}) copy-start(f32[1,10,768]{2,0,1:T(1,128)} %param.19) | copy-start | bytes 92164
  37.4 12.9 %collective-permute-start.4 = (bf16[224,768]{1,0:T(8,128)(2,1)S(1)}, bf16[224,768]{1,0:T(8,128)(2,1)S(1)}, u32[]{:S(2)}, u32[]{:S(2)}) collective-permute-start(bf16[224,768]{1,0:T(8,128)(2,1)S(1)} %pad_maximum_fusion.1), channel_id=1, source_target_pairs={{0,2},{2,0},{1,3},{3,1},{4,6},{6,4},{5,7},{7,5},{8,10},{10,8},{9,1... | collective-permute-start | bytes 1032200 | tf_op jit(solution)/shard_map/ppermute | solution.py:880
  39.1 15.7 %collective-permute-start.3 = (bf16[224,768]{1,0:T(8,128)(2,1)S(1)}, bf16[224,768]{1,0:T(8,128)(2,1)S(1)}, u32[]{:S(2)}, u32[]{:S(2)}) collective-permute-start(bf16[224,768]{1,0:T(8,128)(2,1)S(1)} %pad_maximum_fusion), channel_id=1, source_target_pairs={{0,4},{4,0},{1,5},{5,1},{2,6},{6,2},{3,7},{7,3},{8,12},{12,8},{9,1... | collective-permute-start | bytes 1032200 | tf_op jit(solution)/shard_map/ppermute | solution.py:880
  50.4 4.5 %copy-start.17 = (bf16[224,768]{1,0:T(8,128)(2,1)}, bf16[224,768]{1,0:T(8,128)(2,1)S(1)}, u32[]{:S(2)}) copy-start(bf16[224,768]{1,0:T(8,128)(2,1)S(1)} %collective-permute-done.4) | copy-start | bytes 1032196
  54.8 22.1 %copy-start.1 = (bf16[448,768]{1,0:T(8,128)(2,1)}, bf16[448,768]{1,0:T(8,128)(2,1)S(1)}, u32[]{:S(2)}) copy-start(bf16[448,768]{1,0:T(8,128)(2,1)S(1)} %constant_dynamic-update-slice_fusion.2.refs_0_.refs_3_) | copy-start | bytes 2064388
  54.8 11.0 %collective-permute-start.5 = (bf16[448,768]{1,0:T(8,128)(2,1)S(1)}, bf16[448,768]{1,0:T(8,128)(2,1)S(1)}, u32[]{:S(2)}, u32[]{:S(2)}) collective-permute-start(bf16[448,768]{1,0:T(8,128)(2,1)S(1)} %constant_dynamic-update-slice_fusion.2.refs_0_.refs_3_), channel_id=1, source_target_pairs={{0,2},{2,0},{1,3},{3,1},{4,6},{6,4},{5,7},{7,5},{8,10},{10,8},{9,1... | collective-permute-start | bytes 2064392 | tf_op jit(solution)/shard_map/ppermute | solution.py:880
  55.5 21.4 %copy-start = (bf16[448,768]{1,0:T(8,128)(2,1)}, bf16[448,768]{1,0:T(8,128)(2,1)S(1)}, u32[]{:S(2)}) copy-start(bf16[448,768]{1,0:T(8,128)(2,1)S(1)} %constant_dynamic-update-slice_fusion.6.refs_2_.refs_5_) | copy-start | bytes 2064388
  55.5 14.7 %collective-permute-start.6 = (bf16[448,768]{1,0:T(8,128)(2,1)S(1)}, bf16[448,768]{1,0:T(8,128)(2,1)S(1)}, u32[]{:S(2)}, u32[]{:S(2)}) collective-permute-start(bf16[448,768]{1,0:T(8,128)(2,1)S(1)} %constant_dynamic-update-slice_fusion.6.refs_2_.refs_5_), channel_id=1, source_target_pairs={{0,4},{4,0},{1,5},{5,1},{2,6},{6,2},{3,7},{7,3},{8,12},{12,8},{9,1... | collective-permute-start | bytes 2064392 | tf_op jit(solution)/shard_map/ppermute | solution.py:880
  58.1 12.2 %collective-permute-start.7 = (bf16[448,768]{1,0:T(8,128)(2,1)S(1)}, bf16[448,768]{1,0:T(8,128)(2,1)}, u32[]{:S(2)}, u32[]{:S(2)}) collective-permute-start(bf16[448,768]{1,0:T(8,128)(2,1)S(1)} %constant_dynamic-update-slice_fusion.2.refs_0_.refs_3_), channel_id=1, source_target_pairs={{0,1},{1,0},{2,3},{3,2},{4,5},{5,4},{6,7},{7,6},{8,9},{9,8},{10,11... | collective-permute-start | bytes 2064392 | tf_op jit(solution)/shard_map/ppermute | solution.py:880
  61.7 9.5 %collective-permute-start.9 = (bf16[448,768]{1,0:T(8,128)(2,1)S(1)}, bf16[448,768]{1,0:T(8,128)(2,1)S(1)}, u32[]{:S(2)}, u32[]{:S(2)}) collective-permute-start(bf16[448,768]{1,0:T(8,128)(2,1)S(1)} %constant_dynamic-update-slice_fusion.6.refs_2_.refs_5_), channel_id=1, source_target_pairs={{0,1},{1,0},{2,3},{3,2},{4,5},{5,4},{6,7},{7,6},{8,9},{9,8},{10,11... | collective-permute-start | bytes 2064392 | tf_op jit(solution)/shard_map/ppermute | solution.py:880
  65.8 5.4 %copy-start.2 = (bf16[448,768]{1,0:T(8,128)(2,1)}, bf16[448,768]{1,0:T(8,128)(2,1)S(1)}, u32[]{:S(2)}) copy-start(bf16[448,768]{1,0:T(8,128)(2,1)S(1)} %collective-permute-done.5.refs_1_.refs_4_) | copy-start | bytes 2064388
  65.8 5.4 %collective-permute-start.8 = (bf16[448,768]{1,0:T(8,128)(2,1)S(1)}, bf16[448,768]{1,0:T(8,128)(2,1)S(1)}, u32[]{:S(2)}, u32[]{:S(2)}) collective-permute-start(bf16[448,768]{1,0:T(8,128)(2,1)S(1)} %collective-permute-done.5.refs_1_.refs_4_), channel_id=1, source_target_pairs={{0,1},{1,0},{2,3},{3,2},{4,5},{5,4},{6,7},{7,6},{8,9},{9,8},{10,11... | collective-permute-start | bytes 2064392 | tf_op jit(solution)/shard_map/ppermute | solution.py:880
  70.2 2.1 collective-permute-start.10
  230.7 10.4 %copy-start.30 = (f32[8,768]{1,0:T(8,128)S(1)}, f32[8,768]{1,0:T(8,128)}, u32[]{:S(2)}) copy-start(f32[8,768]{1,0:T(8,128)} %get-tuple-element.123) | copy-start | bytes 73732
  230.7 10.4 %copy-start.31 = (f32[4,768]{1,0:T(4,128)S(1)}, f32[4,768]{1,0:T(4,128)}, u32[]{:S(2)}) copy-start(f32[4,768]{1,0:T(4,128)} %get-tuple-element.125) | copy-start | bytes 36868
  230.8 10.5 %copy-start.28 = (f32[10,768]{1,0:T(8,128)S(1)}, f32[10,768]{1,0:T(8,128)}, u32[]{:S(2)}) copy-start(f32[10,768]{1,0:T(8,128)} %get-tuple-element.124) | copy-start | bytes 92164
  240.8 18.2 %collective-permute-start.11 = (bf16[2,768,768]{2,1,0:T(8,128)(2,1)}, bf16[2,768,768]{2,1,0:T(8,128)(2,1)}, u32[]{:S(2)}, u32[]{:S(2)}) collective-permute-start(bf16[2,768,768]{2,1,0:T(8,128)(2,1)} %shard_map.164), channel_id=1, source_target_pairs={{0,1},{1,0},{2,3},{3,2},{4,5},{5,4},{6,7},{7,6},{8,9},{9,8},{10,11... | collective-permute-start | bytes 7077896 | tf_op jit(solution)/shard_map/ppermute | solution.py:880
  259.0 29.0 %collective-permute-start.14 = (bf16[2,8,112,768]{3,2,1,0:T(8,128)(2,1)}, bf16[2,8,112,768]{3,2,1,0:T(8,128)(2,1)}, u32[]{:S(2)}, u32[]{:S(2)}) collective-permute-start(bf16[2,8,112,768]{3,2,1,0:T(8,128)(2,1)} %get-tuple-element.132), channel_id=1, source_target_pairs={{0,1},{1,0},{2,3},{3,2},{4,5},{5,4},{6,7},{7,6},{8,9},{9,8},{10,11... | collective-permute-start | bytes 8257544 | tf_op jit(solution)/shard_map/ppermute | solution.py:880
  263.1 24.9 %collective-permute-start.12 = (bf16[2,2,96,768]{3,2,1,0:T(8,128)(2,1)}, bf16[2,2,96,768]{3,2,1,0:T(8,128)(2,1)S(1)}, u32[]{:S(2)}, u32[]{:S(2)}) collective-permute-start(bf16[2,2,96,768]{3,2,1,0:T(8,128)(2,1)} %get-tuple-element.130), channel_id=1, source_target_pairs={{0,4},{4,0},{1,5},{5,1},{2,6},{6,2},{3,7},{7,3},{8,12},{12,8},{9,1... | collective-permute-start | bytes 1769480 | tf_op jit(solution)/shard_map/ppermute | solution.py:880
  264.7 23.3 %collective-permute-start.13 = (bf16[2,2,96,768]{3,2,1,0:T(8,128)(2,1)}, bf16[2,2,96,768]{3,2,1,0:T(8,128)(2,1)S(1)}, u32[]{:S(2)}, u32[]{:S(2)}) collective-permute-start(bf16[2,2,96,768]{3,2,1,0:T(8,128)(2,1)} %get-tuple-element.131), channel_id=1, source_target_pairs={{0,2},{2,0},{1,3},{3,1},{4,6},{6,4},{5,7},{7,5},{8,10},{10,8},{9,1... | collective-permute-start | bytes 1769480 | tf_op jit(solution)/shard_map/ppermute | solution.py:880
  288.0 29.5 %collective-permute-start.19 = (bf16[4,4,96,768]{3,2,1,0:T(8,128)(2,1)}, bf16[4,4,96,768]{3,2,1,0:T(8,128)(2,1)}, u32[]{:S(2)}, u32[]{:S(2)}) collective-permute-start(bf16[4,4,96,768]{3,2,1,0:T(8,128)(2,1)} %get-tuple-element.149), channel_id=1, source_target_pairs={{0,1},{1,0},{2,3},{3,2},{4,5},{5,4},{6,7},{7,6},{8,9},{9,8},{10,11... | collective-permute-start | bytes 7077896 | tf_op jit(solution)/shard_map/ppermute | solution.py:880
  293.2 24.3 %collective-permute-start.17 = (bf16[2,2,112,768]{3,2,1,0:T(8,128)(2,1)}, bf16[2,2,112,768]{3,2,1,0:T(8,128)(2,1)S(1)}, u32[]{:S(2)}, u32[]{:S(2)}) collective-permute-start(bf16[2,2,112,768]{3,2,1,0:T(8,128)(2,1)} %get-tuple-element.147), channel_id=1, source_target_pairs={{0,4},{4,0},{1,5},{5,1},{2,6},{6,2},{3,7},{7,3},{8,12},{12,8},{9,1... | collective-permute-start | bytes 2064392 | tf_op jit(solution)/shard_map/ppermute | solution.py:880
  294.1 23.4 %collective-permute-start.18 = (bf16[2,2,112,768]{3,2,1,0:T(8,128)(2,1)}, bf16[2,2,112,768]{3,2,1,0:T(8,128)(2,1)S(1)}, u32[]{:S(2)}, u32[]{:S(2)}) collective-permute-start(bf16[2,2,112,768]{3,2,1,0:T(8,128)(2,1)} %get-tuple-element.148), channel_id=1, source_target_pairs={{0,2},{2,0},{1,3},{3,1},{4,6},{6,4},{5,7},{7,5},{8,10},{10,8},{9,1... | collective-permute-start | bytes 2064392 | tf_op jit(solution)/shard_map/ppermute | solution.py:880
  295.3 22.2 %collective-permute-start.15 = (bf16[2,96,768]{2,1,0:T(8,128)(2,1)}, bf16[2,96,768]{2,1,0:T(8,128)(2,1)S(1)}, u32[]{:S(2)}, u32[]{:S(2)}) collective-permute-start(bf16[2,96,768]{2,1,0:T(8,128)(2,1)} %get-tuple-element.145), channel_id=1, source_target_pairs={{0,2},{2,0},{1,3},{3,1},{4,6},{6,4},{5,7},{7,5},{8,10},{10,8},{9,1... | collective-permute-start | bytes 884744 | tf_op jit(solution)/shard_map/ppermute | solution.py:880
  296.2 21.4 %collective-permute-start.16 = (bf16[2,96,768]{2,1,0:T(8,128)(2,1)}, bf16[2,96,768]{2,1,0:T(8,128)(2,1)S(1)}, u32[]{:S(2)}, u32[]{:S(2)}) collective-permute-start(bf16[2,96,768]{2,1,0:T(8,128)(2,1)} %get-tuple-element.146), channel_id=1, source_target_pairs={{0,4},{4,0},{1,5},{5,1},{2,6},{6,2},{3,7},{7,3},{8,12},{12,8},{9,1... | collective-permute-start | bytes 884744 | tf_op jit(solution)/shard_map/ppermute | solution.py:880
  323.2 22.4 %collective-permute-start.23 = (bf16[2,2,96,768]{3,2,1,0:T(8,128)(2,1)}, bf16[2,2,96,768]{3,2,1,0:T(8,128)(2,1)S(1)}, u32[]{:S(2)}, u32[]{:S(2)}) collective-permute-start(bf16[2,2,96,768]{3,2,1,0:T(8,128)(2,1)} %get-tuple-element.160), channel_id=1, source_target_pairs={{0,4},{4,0},{1,5},{5,1},{2,6},{6,2},{3,7},{7,3},{8,12},{12,8},{9,1... | collective-permute-start | bytes 1769480 | tf_op jit(solution)/shard_map/ppermute | solution.py:880
  324.4 21.2 %collective-permute-start.24 = (bf16[2,2,96,768]{3,2,1,0:T(8,128)(2,1)}, bf16[2,2,96,768]{3,2,1,0:T(8,128)(2,1)S(1)}, u32[]{:S(2)}, u32[]{:S(2)}) collective-permute-start(bf16[2,2,96,768]{3,2,1,0:T(8,128)(2,1)} %get-tuple-element.161), channel_id=1, source_target_pairs={{0,2},{2,0},{1,3},{3,1},{4,6},{6,4},{5,7},{7,5},{8,10},{10,8},{9,1... | collective-permute-start | bytes 1769480 | tf_op jit(solution)/shard_map/ppermute | solution.py:880
  326.0 19.5 %collective-permute-start.21 = (bf16[2,112,768]{2,1,0:T(8,128)(2,1)}, bf16[2,112,768]{2,1,0:T(8,128)(2,1)S(1)}, u32[]{:S(2)}, u32[]{:S(2)}) collective-permute-start(bf16[2,112,768]{2,1,0:T(8,128)(2,1)} %get-tuple-element.158), channel_id=1, source_target_pairs={{0,2},{2,0},{1,3},{3,1},{4,6},{6,4},{5,7},{7,5},{8,10},{10,8},{9,1... | collective-permute-start | bytes 1032200 | tf_op jit(solution)/shard_map/ppermute | solution.py:880
  326.4 19.1 %collective-permute-start.22 = (bf16[2,112,768]{2,1,0:T(8,128)(2,1)}, bf16[2,112,768]{2,1,0:T(8,128)(2,1)S(1)}, u32[]{:S(2)}, u32[]{:S(2)}) collective-permute-start(bf16[2,112,768]{2,1,0:T(8,128)(2,1)} %get-tuple-element.159), channel_id=1, source_target_pairs={{0,4},{4,0},{1,5},{5,1},{2,6},{6,2},{3,7},{7,3},{8,12},{12,8},{9,1... | collective-permute-start | bytes 1032200 | tf_op jit(solution)/shard_map/ppermute | solution.py:880
  327.3 8.2 %collective-permute-start.20 = (bf16[96,768]{1,0:T(8,128)(2,1)}, bf16[96,768]{1,0:T(8,128)(2,1)S(1)}, u32[]{:S(2)}, u32[]{:S(2)}) collective-permute-start(bf16[96,768]{1,0:T(8,128)(2,1)} %get-tuple-element.157), channel_id=1, source_target_pairs={{0,16},{8,24},{16,0},{24,8},{1,17},{9,25},{17,1},{25,9},{2,18},{10... | collective-permute-start | bytes 442376 | tf_op jit(solution)/shard_map/ppermute | solution.py:880
  335.5 10.1 %copy-start.25 = (bf16[96,768]{1,0:T(8,128)(2,1)}, bf16[96,768]{1,0:T(8,128)(2,1)S(1)}, u32[]{:S(2)}) copy-start(bf16[96,768]{1,0:T(8,128)(2,1)S(1)} %collective-permute-done.20) | copy-start | bytes 442372
  346.8 10.5 %copy-start.27 = (f32[10,768]{1,0:T(8,128)S(1)}, f32[10,768]{1,0:T(8,128)}, u32[]{:S(2)}) copy-start(f32[10,768]{1,0:T(8,128)} %get-tuple-element.176) | copy-start | bytes 92164
  351.6 22.7 %collective-permute-start.25 = (bf16[208,768]{1,0:T(8,128)(2,1)}, bf16[208,768]{1,0:T(8,128)(2,1)S(1)}, u32[]{:S(2)}, u32[]{:S(2)}) collective-permute-start(bf16[208,768]{1,0:T(8,128)(2,1)} %get-tuple-element.168), channel_id=1, source_target_pairs={{0,8},{8,0},{16,24},{24,16},{1,9},{9,1},{17,25},{25,17},{2,10},{10... | collective-permute-start | bytes 958472 | tf_op jit(solution)/shard_map/ppermute | solution.py:880
  351.7 22.7 %collective-permute-start.26 = (bf16[208,768]{1,0:T(8,128)(2,1)}, bf16[208,768]{1,0:T(8,128)(2,1)S(1)}, u32[]{:S(2)}, u32[]{:S(2)}) collective-permute-start(bf16[208,768]{1,0:T(8,128)(2,1)} %get-tuple-element.169), channel_id=1, source_target_pairs={{0,24},{8,16},{16,8},{24,0},{1,25},{9,17},{17,9},{25,1},{2,26},{10... | collective-permute-start | bytes 958472 | tf_op jit(solution)/shard_map/ppermute | solution.py:880
  354.6 19.8 %collective-permute-start.28 = (bf16[2,96,768]{2,1,0:T(8,128)(2,1)}, bf16[2,96,768]{2,1,0:T(8,128)(2,1)S(1)}, u32[]{:S(2)}, u32[]{:S(2)}) collective-permute-start(bf16[2,96,768]{2,1,0:T(8,128)(2,1)} %get-tuple-element.171), channel_id=1, source_target_pairs={{0,2},{2,0},{1,3},{3,1},{4,6},{6,4},{5,7},{7,5},{8,10},{10,8},{9,1... | collective-permute-start | bytes 884744 | tf_op jit(solution)/shard_map/ppermute | solution.py:880
  356.3 18.1 %collective-permute-start.29 = (bf16[2,96,768]{2,1,0:T(8,128)(2,1)}, bf16[2,96,768]{2,1,0:T(8,128)(2,1)S(1)}, u32[]{:S(2)}, u32[]{:S(2)}) collective-permute-start(bf16[2,96,768]{2,1,0:T(8,128)(2,1)} %get-tuple-element.172), channel_id=1, source_target_pairs={{0,4},{4,0},{1,5},{5,1},{2,6},{6,2},{3,7},{7,3},{8,12},{12,8},{9,1... | collective-permute-start | bytes 884744 | tf_op jit(solution)/shard_map/ppermute | solution.py:880
  356.8 17.5 %collective-permute-start.27 = (bf16[112,768]{1,0:T(8,128)(2,1)}, bf16[112,768]{1,0:T(8,128)(2,1)S(1)}, u32[]{:S(2)}, u32[]{:S(2)}) collective-permute-start(bf16[112,768]{1,0:T(8,128)(2,1)} %get-tuple-element.170), channel_id=1, source_target_pairs={{0,16},{8,24},{16,0},{24,8},{1,17},{9,25},{17,1},{25,9},{2,18},{10... | collective-permute-start | bytes 516104 | tf_op jit(solution)/shard_map/ppermute | solution.py:880
  357.9 16.5 %copy-start.23 = (bf16[112,768]{1,0:T(8,128)(2,1)S(1)}, bf16[112,768]{1,0:T(8,128)(2,1)}, u32[]{:S(2)}) copy-start(bf16[112,768]{1,0:T(8,128)(2,1)} %get-tuple-element.184) | copy-start | bytes 516100
  375.5 8.4 %copy-start.24 = (bf16[96,768]{1,0:T(8,128)(2,1)S(1)}, bf16[96,768]{1,0:T(8,128)(2,1)}, u32[]{:S(2)}) copy-start(bf16[96,768]{1,0:T(8,128)(2,1)} %get-tuple-element.188) | copy-start | bytes 442372
  375.5 8.4 %copy-start.26 = (bf16[96,768]{1,0:T(8,128)(2,1)S(1)}, bf16[96,768]{1,0:T(8,128)(2,1)}, u32[]{:S(2)}) copy-start(bf16[96,768]{1,0:T(8,128)(2,1)} %copy-done.25) | copy-start | bytes 442372
  378.8 7.8 %collective-permute-start.30 = (bf16[96,768]{1,0:T(8,128)(2,1)}, bf16[96,768]{1,0:T(8,128)(2,1)S(1)}, u32[]{:S(2)}, u32[]{:S(2)}) collective-permute-start(bf16[96,768]{1,0:T(8,128)(2,1)} %get-tuple-element.181), channel_id=1, source_target_pairs={{0,8},{8,0},{16,24},{24,16},{1,9},{9,1},{17,25},{25,17},{2,10},{10... | collective-permute-start | bytes 442376 | tf_op jit(solution)/shard_map/ppermute | solution.py:880
  378.9 12.0 %collective-permute-start.31 = (bf16[96,768]{1,0:T(8,128)(2,1)}, bf16[96,768]{1,0:T(8,128)(2,1)S(1)}, u32[]{:S(2)}, u32[]{:S(2)}) collective-permute-start(bf16[96,768]{1,0:T(8,128)(2,1)} %get-tuple-element.182), channel_id=1, source_target_pairs={{0,16},{8,24},{16,0},{24,8},{1,17},{9,25},{17,1},{25,9},{2,18},{10... | collective-permute-start | bytes 442376 | tf_op jit(solution)/shard_map/ppermute | solution.py:880
  382.1 8.9 %collective-permute-start.32 = (bf16[96,768]{1,0:T(8,128)(2,1)}, bf16[96,768]{1,0:T(8,128)(2,1)S(1)}, u32[]{:S(2)}, u32[]{:S(2)}) collective-permute-start(bf16[96,768]{1,0:T(8,128)(2,1)} %get-tuple-element.183), channel_id=1, source_target_pairs={{0,24},{8,16},{16,8},{24,0},{1,25},{9,17},{17,9},{25,1},{2,26},{10... | collective-permute-start | bytes 442376 | tf_op jit(solution)/shard_map/ppermute | solution.py:880
  (18 other events, 20.7 us)
Sparse Core Ops, SparseCore 0:
  11.5 92.6 all-gather.1
where the time goes:
time: 407 us; the launch traced here: 400 us
  Pallas kernels  238 us (58%)
  waiting for transfers between devices  67.4 us (17%)
  local copies, waits for them, and re-layouts  37.9 us (9%)
  starting transfers between devices  33.5 us (8%)
  between operations  16.5 us (4%)
  other arithmetic  6.79 us (2%)
    pallas_call x1, Pallas kernels, backward_call(): pl.pallas_call(functools.partial(backward_kernel, plan, len(pieces)), gri...  73.2 us
    ppermute x33, waiting for transfers between devices, swap(): return lax.ppermute(value, axis, [(i, i ^ mask) for i in range(size)])  67.4 us
    pallas_call x1, Pallas kernels, forward_call(): pl.pallas_call(functools.partial(forward_kernel, plan, len(pieces)), grid...  51.1 us
    pallas_call x3, Pallas kernels, __call__(): pl.pallas_call(functools.partial(self.kernel, len(arrays), len(out_shapes...  49.1 us
    ppermute x33, starting transfers between devices, swap(): return lax.ppermute(value, axis, [(i, i ^ mask) for i in range(size)])  33.5 us
    pallas_call x1, Pallas kernels, early_call(): pl.pallas_call(functools.partial(early_kernel, plan, len(pieces)), grid=(...  29.5 us
    pallas_call x5, Pallas kernels, deal(): pl.pallas_call(functools.partial(deal_kernel, plain, places, len(arrays),...  19.9 us
    pallas_call x1, Pallas kernels, text_grad_call(): pl.pallas_call(functools.partial(text_grad_kernel, plan, len(pieces)), gr...  15 us
  transfers between devices with their start and end apart: 34, of which 11 were waited for; matrix products, arithmetic and copies ran while one was open for 9% of the time, Pallas kernels for 23%

commit v1 on v0

--- a/solution.py
+++ b/solution.py
@@ -568,8 +568,8 @@
         outputs, refs = refs[:n_out], refs[n_out:]
         held, refs = refs[:n_loads], refs[n_loads:]
         results, refs = refs[:n_jobs], refs[n_jobs:]
-        load_sem, store_sem = refs[:2]
-        weights, weight_sem = refs[2:3], refs[3:]
+        load_sem, store_sem, partial = refs[:3]
+        weights, weight_sem = refs[3:4], refs[4:]
         step = pl.program_id(0)
 
         def load(n):
@@ -582,6 +582,15 @@
                     place = index_ref[kind[1]] if kind[0] == "index" else kind[1]
                     view = view.at[:, pl.ds(pl.multiple_of(place * self.block, 128), self.block)]
             return pltpu.make_async_copy(view, held[n], load_sem.at[n])
+
+        def half(n, part):
+            source, kind = self.loads[n]
+            rows = held[n].shape[0] // 2
+            view = inputs[source].at[pl.ds(part * rows, rows), :]
+            if kind is not None:
+                place = index_ref[kind[1]] if kind[0] == "index" else kind[1]
+                view = inputs[source].at[pl.ds(part * rows, rows), pl.ds(pl.multiple_of(place * self.block, 128), self.block)]
+            return pltpu.make_async_copy(view, held[n].at[pl.ds(part * rows, rows), :], load_sem.at[n if part else n_loads + n])
 
         needs = [[self.loads.index(x) for x in loads] for _, loads, _ in self.jobs]
         fresh, seen = [], set()
@@ -617,18 +626,36 @@
             def _():
                 if n == 0:
                     for m in fresh[0]:
-                        load(m).start()
+                        half(m, 0).start()
                 if output[0] == "packed":
                     shared_rows(n).start()
                 for m in fresh[n]:
-                    load(m).wait()
-                for m in fresh[n + 1] if n + 1 < n_jobs else ():
-                    load(m).start()
+                    (load(m) if n else half(m, 0)).wait()
+                if n == 0:
+                    for m in fresh[0]:
+                        half(m, 1).start()
+                else:
+                    for m in fresh[n + 2] if n + 2 < n_jobs else ():
+                        load(m).start()
                 texts = [m for m, job in enumerate(self.jobs) if job[0] == "text"]
                 if texts and n == texts[0] - 1:
                     start_loads(table_ref, pieces, self.plan, weights, weight_sem[0], (0,))
                 if texts and n == texts[0]:
                     wait_loads(weights, weight_sem[0], 0)
+
+            if n == 0:
+
+                @pl.when(step == 0)
+                def _():
+                    rows = held[0].shape[0] // 2
+                    partial[...] = dot_tn(held[needs[0][0]][:rows, :], held[needs[0][1]][:rows, :])
+
+                @pl.when(step == 0)
+                def _():
+                    for m in fresh[0]:
+                        half(m, 1).wait()
+                    for m in sum(fresh[1:3], []):
+                        load(m).start()
 
             @pl.when(step == n)
             def _():
@@ -643,7 +670,12 @@
                     outputs[output[1]][0] = results[n][:TEXT, :]
                 else:
                     left, right = needs[n]
-                    value = {"tn": dot_tn, "nn": dot_nn}[form](held[left][...], held[right][...]).astype(bf16)
+                    if n == 0:
+                        rows = held[left].shape[0] // 2
+                        value = partial[...] + dot_tn(held[left][rows:, :], held[right][rows:, :])
+                    else:
+                        value = {"tn": dot_tn, "nn": dot_nn}[form](held[left][...], held[right][...])
+                    value = value.astype(bf16)
                     if output[0] == "packed":
                         items, rows, _ = results[n].shape
                         shard = rows - self.small[2]
@@ -675,7 +707,11 @@
             else:
                 scratch.append(pltpu.VMEM((width // own, own, block) if kind == "split" else (width, block), bf16))
             self.store_counts.append({"split": width // own, "text": 0}.get(kind, 1))
-        scratch += [pltpu.SemaphoreType.DMA((len(self.loads),)), pltpu.SemaphoreType.DMA((sum(self.store_counts) + len(self.jobs),))]
+        scratch += [
+            pltpu.SemaphoreType.DMA((2 * len(self.loads),)),
+            pltpu.SemaphoreType.DMA((sum(self.store_counts) + len(self.jobs),)),
+            pltpu.VMEM((width, block), f32),
+        ]
         if pieces:
             scratch += [pltpu.VMEM((4 * width, width), bf16), pltpu.SemaphoreType.DMA((1,))]
         ahead = len(self.jobs) - SEGS_MAX

time: 407 us -> 406 us (level)
  transfers between devices with their start and end apart: 34 -> 34, of which waited for: 11 -> 11; matrix products, arithmetic and copies ran while one was open for 9% -> 9% of each run, Pallas kernels for 23% -> 22%
where the time goes in v1:
time: 406 us; the launch traced here: 398 us
  Pallas kernels  236 us (58%)
  waiting for transfers between devices  67.1 us (17%)
  local copies, waits for them, and re-layouts  37.9 us (9%)
  starting transfers between devices  33.7 us (8%)
  between operations  16.5 us (4%)
  other arithmetic  6.79 us (2%)
    pallas_call x1, Pallas kernels, backward_call(): pl.pallas_call(functools.partial(backward_kernel, plan, len(pieces)), gri...  73.2 us
    ppermute x33, waiting for transfers between devices, swap(): return lax.ppermute(value, axis, [(i, i ^ mask) for i in range(size)])  67 us
    pallas_call x1, Pallas kernels, forward_call(): pl.pallas_call(functools.partial(forward_kernel, plan, len(pieces)), grid...  51.1 us
    pallas_call x3, Pallas kernels, __call__(): pl.pallas_call(functools.partial(self.kernel, len(arrays), len(out_shapes...  47.7 us
    ppermute x33, starting transfers between devices, swap(): return lax.ppermute(value, axis, [(i, i ^ mask) for i in range(size)])  33.6 us
    pallas_call x1, Pallas kernels, early_call(): pl.pallas_call(functools.partial(early_kernel, plan, len(pieces)), grid=(...  29.5 us
    pallas_call x5, Pallas kernels, deal(): pl.pallas_call(functools.partial(deal_kernel, plain, places, len(arrays),...  19.9 us
    pallas_call x1, Pallas kernels, text_grad_call(): pl.pallas_call(functools.partial(text_grad_kernel, plan, len(pieces)), gr...  15 us
  transfers between devices with their start and end apart: 34, of which 11 were waited for; matrix products, arithmetic and copies ran while one was open for 9% of the time, Pallas kernels for 22%

profile of v1, /device:TPU:0, one launch (start us, length us, event | category | flops | bytes accessed | tf_op | source)
XLA Modules:
  0.0 398.2 jit_solution(7122978067458704037)
XLA Ops:
  7.2 1.7 pad_maximum_fusion.2
  10.5 0.9 constant_dynamic-update-slice_fusion.5
  11.5 5.1 %collective-permute-start.2 = (bf16[112,768]{1,0:T(8,128)(2,1)S(1)}, bf16[112,768]{1,0:T(8,128)(2,1)S(1)}, u32[]{:S(2)}, u32[]{:S(2)}) collective-permute-start(bf16[112,768]{1,0:T(8,128)(2,1)S(1)} %get-tuple-element.253), channel_id=1, source_target_pairs={{0,24},{8,16},{16,8},{24,0},{1,25},{9,17},{17,9},{25,1},{2,26},{10... | collective-permute-start | bytes 516104 | tf_op jit(solution)/shard_map/ppermute | solution.py:916
  17.2 4.0 %copy.77 = bf16[1,4,502,768]{3,2,1,0:T(8,128)(2,1)} copy(bf16[1,4,502,768]{3,1,2,0:T(4,128)(2,1)} %param.10) | data formatting | bytes 6168576 | tf_op args[0]
  21.3 2.0 copy.76
  23.4 1.6 sort.17
  25.0 12.4 %collective-permute-done.1 = bf16[112,768]{1,0:T(8,128)(2,1)S(1)} collective-permute-done((bf16[112,768]{1,0:T(8,128)(2,1)S(1)}, bf16[112,768]{1,0:T(8,128)(2,1)S(1)}, u32[]{:S(2)}, u32[]{:S(2)}) %collective-permute-start.1) | collective-permute-done | bytes 172064 | tf_op jit(solution)/shard_map/ppermute | solution.py:916
  37.4 1.6 collective-permute-start.4
  39.1 1.6 collective-permute-start.3
  40.7 9.7 %collective-permute-done.4 = bf16[224,768]{1,0:T(8,128)(2,1)S(1)} collective-permute-done((bf16[224,768]{1,0:T(8,128)(2,1)S(1)}, bf16[224,768]{1,0:T(8,128)(2,1)S(1)}, u32[]{:S(2)}, u32[]{:S(2)}) %collective-permute-start.4) | collective-permute-done | bytes 344096 | tf_op jit(solution)/shard_map/ppermute | solution.py:916
  50.4 4.4 %collective-permute-done.3 = bf16[224,768]{1,0:T(8,128)(2,1)S(1)} collective-permute-done((bf16[224,768]{1,0:T(8,128)(2,1)S(1)}, bf16[224,768]{1,0:T(8,128)(2,1)S(1)}, u32[]{:S(2)}, u32[]{:S(2)}) %collective-permute-start.3) | collective-permute-done | bytes 344096 | tf_op jit(solution)/shard_map/ppermute | solution.py:916
  55.5 2.5 collective-permute-start.6
  63.0 2.8 collective-permute-done.5.refs_1_.refs_4_
  65.8 4.4 %collective-permute-done.6.refs_3_.refs_6_ = bf16[448,768]{1,0:T(8,128)(2,1)S(1)} collective-permute-done((bf16[448,768]{1,0:T(8,128)(2,1)S(1)}, bf16[448,768]{1,0:T(8,128)(2,1)S(1)}, u32[]{:S(2)}, u32[]{:S(2)}) %collective-permute-start.6) | collective-permute-done | bytes 688160 | tf_op jit(solution)/shard_map/ppermute | solution.py:916
  70.2 0.9 fusion.9
  71.3 1.1 collective-permute-done.10.refs_7_.refs_10_
  76.0 1.0 copy.61
  76.9 29.5 %shard_map.161 = (bf16[2304,2048]{1,0:T(8,128)(2,1)}, bf16[768,2048]{1,0:T(8,128)(2,1)}, f32[4,16,512]{2,1,0:T(8,128)}) custom-call(s32[1]{0:T(128)S(6)} %copy.86.count_ref, s32[1]{0:T(128)S(6)} %copy.87.fill_ref, s32[96]{0:T(128)} %stack.322.table_ref, bf16[4,502,768]{2,1,0:T(8,128)(2,1)} %bitcast.153, f32[768,2]{1,0:T(8,128)} %bitcast.161, ...), custom_call_target="tpu_custom_call" | custom-call | tf_op jit(solution)/shard_map/pallas_call | solution.py:173
  106.5 51.1 %shard_map.162 = (bf16[4,502,768]{2,1,0:T(8,128)(2,1)}, f32[10,768]{1,0:T(8,128)}, bf16[2048,768]{1,0:T(8,128)(2,1)}, bf16[2304,2048]{1,0:T(8,128)(2,1)}, bf16[7...) custom-call(s32[1]{0:T(128)S(6)} %copy.86.count_ref, ...), custom_call_target="tpu_custom_call" | custom-call | tf_op jit(solution)/shard_map/pallas_call | solution.py:473
  157.5 73.2 %shard_map.163 = (f32[2048,768]{1,0:T(8,128)}, bf16[2048,768]{1,0:T(8,128)(2,1)}, bf16[2048,3072]{1,0:T(8,128)(2,1)}, bf16[2048,768]{1,0:T(8,128)(2,1)}, bf16[20...) custom-call(s32[1]{0:T(128)S(6)} %copy.86.count_ref, s32[1]{0:T(128)S(6)} %copy.87.fill_ref, ...), custom_call_target="tpu_custom_call" | custom-call | tf_op jit(solution)/shard_map/pallas_call | solution.py:521
  230.8 10.2 %shard_map.164 = bf16[2,768,768]{2,1,0:T(8,128)(2,1)} custom-call(s32[5]{0:T(128)} %stack.289.index_ref.table_ref, s32[5]{0:T(128)} %stack.289.index_ref.table_ref, bf16[2048,768]{1,0:T(8,128)(2,1)} %get-tuple-element.120.refs_0_, bf16[2048,3072]{1,0:T(8,128)(2,1)} %get-tuple-element.119.refs_1_), custom_call_target="tpu_custom_call" | custom-call | tf_op jit(solution)/shard_map/pallas_call | solution.py:719
  241.9 1.0 copy.69
  242.9 15.7 %shard_map.165 = (bf16[2,768,768]{2,1,0:T(8,128)(2,1)}, bf16[2,8,112,768]{3,2,1,0:T(8,128)(2,1)}) custom-call(s32[5]{0:T(128)} %stack.289.index_ref.table_ref, s32[5]{0:T(128)} %stack.289.index_ref.table_ref, bf16[2048,768]{1,0:T(8,128)(2,1)} %get-tuple-element.120.refs_0_, bf16[2048,3072]{1,0:T(8,128)(2,1)} %get-tuple-element.119.refs_1_, ...), custom_call_target="tpu_custom_call" | custom-call | tf_op jit(solution)/shard_map/pallas_call | solution.py:719
  259.7 3.2 shard_map.166
  262.9 1.7 collective-permute-start.12
  264.9 21.8 %shard_map.167 = (bf16[2,8,112,768]{3,2,1,0:T(8,128)(2,1)}, bf16[4,4,96,768]{3,2,1,0:T(8,128)(2,1)}, bf16[4,4,96,768]{3,2,1,0:T(8,128)(2,1)}) custom-call(s32[5]{0:T(128)} %stack.289.index_ref.table_ref, s32[5]{0:T(128)} %stack.289.index_ref.table_ref, bf16[2048,768]{1,0:T(8,128)(2,1)} %get-tuple-element.133.refs_2_.refs_0_, ...), custom_call_target="tpu_custom_call" | custom-call | tf_op jit(solution)/shard_map/pallas_call | solution.py:719
  287.8 4.1 %shard_map.168 = (bf16[2,96,768]{2,1,0:T(8,128)(2,1)}, bf16[2,96,768]{2,1,0:T(8,128)(2,1)}, bf16[2,2,112,768]{3,2,1,0:T(8,128)(2,1)}, bf16[2,2,112,768]{3,2,1,0:T(8,128)(2,1)}) custom-call(s32[16]{0:T(128)} %stack.284.index_ref, bf16[2,4,2,96,768]{4,3,2,1,0:T(8,128)(2,1)} %bitcast.135, ...), custom_call_target="tpu_custom_call" | custom-call | tf_op jit(solution)/shard_map/pallas_call | solution.py:849
  292.0 0.9 collective-permute-start.17
  292.9 1.3 collective-permute-start.18
  294.9 1.2 collective-permute-start.16
  296.1 15.0 %shard_map.169 = f32[4,502,768]{2,1,0:T(8,128)} custom-call(s32[96]{0:T(128)} %stack.322.table_ref, f32[2048,768]{1,0:T(8,128)} %get-tuple-element.151.first_ref, bf16[2048,2304]{1,0:T(8,128)(2,1)} %get-tuple-element.135.refs_3_.gqkv_ref, bf16[448,768]{1,0:T(8,128)(2,1)} %copy-done.1, bf16[448,768]{1,0:T(8,128)(2,1)} %copy-done.2, bf16[448,768]{1,0:T(8,128)(2,1)} %copy-done, ...), custom_call_target="tpu_custom_call" | custom-call | tf_op jit(solution)/shard_map/pallas_call | solution.py:753
  311.0 5.1 %collective-permute-done.15.refs_16_.refs_20_ = bf16[2,96,768]{2,1,0:T(8,128)(2,1)S(1)} collective-permute-done((bf16[2,96,768]{2,1,0:T(8,128)(2,1)}, bf16[2,96,768]{2,1,0:T(8,128)(2,1)S(1)}, u32[]{:S(2)}, u32[]{:S(2)}) %collective-permute-start.15) | collective-permute-done | bytes 294944 | tf_op jit(solution)/shard_map/ppermute | solution.py:916
  317.4 4.4 %shard_map.170 = (bf16[2,112,768]{2,1,0:T(8,128)(2,1)}, bf16[2,112,768]{2,1,0:T(8,128)(2,1)}, bf16[2,2,96,768]{3,2,1,0:T(8,128)(2,1)}, bf16[2,2,96,768]{3,2,1,0:...) custom-call(s32[16]{0:T(128)} %stack.284.index_ref, bf16[2,4,2,112,768]{4,3,2,1,0:T(8,128)(2,1)} %bitcast.143, ...), custom_call_target="tpu_custom_call" | custom-call | tf_op jit(solution)/shard_map/pallas_call | solution.py:849
  321.8 1.2 collective-permute-start.23
  323.1 1.7 collective-permute-start.24
  326.4 7.8 %copy.75 = f32[4,502,768]{2,0,1:T(4,128)} copy(f32[4,502,768]{2,1,0:T(8,128)} %shard_map.169) | data formatting | bytes 12337152 | tf_op jit(solution)/shard_map/optimization_barrier | solution.py:920
  334.2 9.9 %collective-permute-done.21.refs_12_ = bf16[2,112,768]{2,1,0:T(8,128)(2,1)S(1)} collective-permute-done((bf16[2,112,768]{2,1,0:T(8,128)(2,1)}, bf16[2,112,768]{2,1,0:T(8,128)(2,1)S(1)}, u32[]{:S(2)}, u32[]{:S(2)}) %collective-permute-start.21) | collective-permute-done | bytes 344096 | tf_op jit(solution)/shard_map/ppermute | solution.py:916
  345.4 4.8 %shard_map.171 = (bf16[2,96,768]{2,1,0:T(8,128)(2,1)}, bf16[2,96,768]{2,1,0:T(8,128)(2,1)}, bf16[112,768]{1,0:T(8,128)(2,1)}, bf16[112,768]{1,0:T(8,128)(2,1)}, ...) custom-call(s32[16]{0:T(128)} %stack.284.index_ref, bf16[4,2,2,96,768]{4,3,2,1,0:T(8,128)(2,1)} %bitcast.149, ...), custom_call_target="tpu_custom_call" | custom-call | tf_op jit(solution)/shard_map/pallas_call | solution.py:849
  350.3 2.9 collective-permute-start.26
  353.1 1.7 collective-permute-start.28
  356.5 4.7 %copy.78 = bf16[4,502,768]{2,0,1:T(4,128)(2,1)} copy(bf16[4,502,768]{2,1,0:T(8,128)(2,1)} %get-tuple-element.174) | data formatting | bytes 6168576 | tf_op jit(solution)/shard_map/optimization_barrier | solution.py:920
  361.3 11.5 %collective-permute-done.27 = bf16[112,768]{1,0:T(8,128)(2,1)S(1)} collective-permute-done((bf16[112,768]{1,0:T(8,128)(2,1)}, bf16[112,768]{1,0:T(8,128)(2,1)S(1)}, u32[]{:S(2)}, u32[]{:S(2)}) %collective-permute-start.27) | collective-permute-done | bytes 172064 | tf_op jit(solution)/shard_map/ppermute | solution.py:916
  373.9 3.4 shard_map.172
  377.4 3.2 collective-permute-start.31
  380.5 1.2 collective-permute-start.32
  383.7 1.4 collective-permute-done.30
  385.1 4.3 %collective-permute-done.31 = bf16[96,768]{1,0:T(8,128)(2,1)S(1)} collective-permute-done((bf16[96,768]{1,0:T(8,128)(2,1)}, bf16[96,768]{1,0:T(8,128)(2,1)S(1)}, u32[]{:S(2)}, u32[]{:S(2)}) %collective-permute-start.31) | collective-permute-done | bytes 147488 | tf_op jit(solution)/shard_map/ppermute | solution.py:916
  389.4 1.7 convert_add_fusion.1
  (200 shorter events, 23.3 us)
Async XLA Ops:
  7.2 99.3 %all-gather.2.cloned.1.call-start = ((), (), s32[]{:S(2)}) async-start(), calls=%async_computation | async-start | bytes 9732096 | tf_op jit(solution)/shard_map/all_gather | solution.py:998
  11.5 13.6 %collective-permute-start.2 = (bf16[112,768]{1,0:T(8,128)(2,1)S(1)}, bf16[112,768]{1,0:T(8,128)(2,1)S(1)}, u32[]{:S(2)}, u32[]{:S(2)}) collective-permute-start(bf16[112,768]{1,0:T(8,128)(2,1)S(1)} %get-tuple-element.253), channel_id=1, source_target_pairs={{0,24},{8,16},{16,8},{24,0},{1,25},{9,17},{17,9},{25,1},{2,26},{10... | collective-permute-start | bytes 516104 | tf_op jit(solution)/shard_map/ppermute | solution.py:916
  16.6 20.8 %collective-permute-start.1 = (bf16[112,768]{1,0:T(8,128)(2,1)S(1)}, bf16[112,768]{1,0:T(8,128)(2,1)S(1)}, u32[]{:S(2)}, u32[]{:S(2)}) collective-permute-start(bf16[112,768]{1,0:T(8,128)(2,1)S(1)} %get-tuple-element.253), channel_id=1, source_target_pairs={{0,16},{8,24},{16,0},{24,8},{1,17},{9,25},{17,1},{25,9},{2,18},{10... | collective-permute-start | bytes 516104 | tf_op jit(solution)/shard_map/ppermute | solution.py:916
  16.6 20.8 %collective-permute-start = (bf16[112,768]{1,0:T(8,128)(2,1)S(1)}, bf16[112,768]{1,0:T(8,128)(2,1)S(1)}, u32[]{:S(2)}, u32[]{:S(2)}) collective-permute-start(bf16[112,768]{1,0:T(8,128)(2,1)S(1)} %get-tuple-element.253), channel_id=1, source_target_pairs={{0,8},{8,0},{16,24},{24,16},{1,9},{9,1},{17,25},{25,17},{2,10},{10... | collective-permute-start | bytes 516104 | tf_op jit(solution)/shard_map/ppermute | solution.py:916
  21.3 17.7 %copy-start.16 = (bf16[96,768]{1,0:T(8,128)(2,1)S(1)}, bf16[96,768]{1,0:T(8,128)(2,1)}, u32[]{:S(2)}) copy-start(bf16[96,768]{1,0:T(8,128)(2,1)} %param.11) | copy-start | bytes 442372
  23.3 36.1 %copy-start.29 = (f32[1,10,768]{2,0,1:T(1,128)S(1)}, f32[1,10,768]{2,0,1:T(1,128)}, u32[]{:S(2)}) copy-start(f32[1,10,768]{2,0,1:T(1,128)} %param.19) | copy-start | bytes 92164
  37.4 12.9 %collective-permute-start.4 = (bf16[224,768]{1,0:T(8,128)(2,1)S(1)}, bf16[224,768]{1,0:T(8,128)(2,1)S(1)}, u32[]{:S(2)}, u32[]{:S(2)}) collective-permute-start(bf16[224,768]{1,0:T(8,128)(2,1)S(1)} %pad_maximum_fusion.1), channel_id=1, source_target_pairs={{0,2},{2,0},{1,3},{3,1},{4,6},{6,4},{5,7},{7,5},{8,10},{10,8},{9,1... | collective-permute-start | bytes 1032200 | tf_op jit(solution)/shard_map/ppermute | solution.py:916
  39.1 15.7 %collective-permute-start.3 = (bf16[224,768]{1,0:T(8,128)(2,1)S(1)}, bf16[224,768]{1,0:T(8,128)(2,1)S(1)}, u32[]{:S(2)}, u32[]{:S(2)}) collective-permute-start(bf16[224,768]{1,0:T(8,128)(2,1)S(1)} %pad_maximum_fusion), channel_id=1, source_target_pairs={{0,4},{4,0},{1,5},{5,1},{2,6},{6,2},{3,7},{7,3},{8,12},{12,8},{9,1... | collective-permute-start | bytes 1032200 | tf_op jit(solution)/shard_map/ppermute | solution.py:916
  50.4 4.5 %copy-start.17 = (bf16[224,768]{1,0:T(8,128)(2,1)}, bf16[224,768]{1,0:T(8,128)(2,1)S(1)}, u32[]{:S(2)}) copy-start(bf16[224,768]{1,0:T(8,128)(2,1)S(1)} %collective-permute-done.4) | copy-start | bytes 1032196
  54.8 22.1 %copy-start.1 = (bf16[448,768]{1,0:T(8,128)(2,1)}, bf16[448,768]{1,0:T(8,128)(2,1)S(1)}, u32[]{:S(2)}) copy-start(bf16[448,768]{1,0:T(8,128)(2,1)S(1)} %constant_dynamic-update-slice_fusion.2.refs_0_.refs_3_) | copy-start | bytes 2064388
  54.8 11.0 %collective-permute-start.5 = (bf16[448,768]{1,0:T(8,128)(2,1)S(1)}, bf16[448,768]{1,0:T(8,128)(2,1)S(1)}, u32[]{:S(2)}, u32[]{:S(2)}) collective-permute-start(bf16[448,768]{1,0:T(8,128)(2,1)S(1)} %constant_dynamic-update-slice_fusion.2.refs_0_.refs_3_), channel_id=1, source_target_pairs={{0,2},{2,0},{1,3},{3,1},{4,6},{6,4},{5,7},{7,5},{8,10},{10,8},{9,1... | collective-permute-start | bytes 2064392 | tf_op jit(solution)/shard_map/ppermute | solution.py:916
  55.5 21.4 %copy-start = (bf16[448,768]{1,0:T(8,128)(2,1)}, bf16[448,768]{1,0:T(8,128)(2,1)S(1)}, u32[]{:S(2)}) copy-start(bf16[448,768]{1,0:T(8,128)(2,1)S(1)} %constant_dynamic-update-slice_fusion.6.refs_2_.refs_5_) | copy-start | bytes 2064388
  55.5 14.7 %collective-permute-start.6 = (bf16[448,768]{1,0:T(8,128)(2,1)S(1)}, bf16[448,768]{1,0:T(8,128)(2,1)S(1)}, u32[]{:S(2)}, u32[]{:S(2)}) collective-permute-start(bf16[448,768]{1,0:T(8,128)(2,1)S(1)} %constant_dynamic-update-slice_fusion.6.refs_2_.refs_5_), channel_id=1, source_target_pairs={{0,4},{4,0},{1,5},{5,1},{2,6},{6,2},{3,7},{7,3},{8,12},{12,8},{9,1... | collective-permute-start | bytes 2064392 | tf_op jit(solution)/shard_map/ppermute | solution.py:916
  58.1 12.2 %collective-permute-start.7 = (bf16[448,768]{1,0:T(8,128)(2,1)S(1)}, bf16[448,768]{1,0:T(8,128)(2,1)}, u32[]{:S(2)}, u32[]{:S(2)}) collective-permute-start(bf16[448,768]{1,0:T(8,128)(2,1)S(1)} %constant_dynamic-update-slice_fusion.2.refs_0_.refs_3_), channel_id=1, source_target_pairs={{0,1},{1,0},{2,3},{3,2},{4,5},{5,4},{6,7},{7,6},{8,9},{9,8},{10,11... | collective-permute-start | bytes 2064392 | tf_op jit(solution)/shard_map/ppermute | solution.py:916
  61.7 9.5 %collective-permute-start.9 = (bf16[448,768]{1,0:T(8,128)(2,1)S(1)}, bf16[448,768]{1,0:T(8,128)(2,1)S(1)}, u32[]{:S(2)}, u32[]{:S(2)}) collective-permute-start(bf16[448,768]{1,0:T(8,128)(2,1)S(1)} %constant_dynamic-update-slice_fusion.6.refs_2_.refs_5_), channel_id=1, source_target_pairs={{0,1},{1,0},{2,3},{3,2},{4,5},{5,4},{6,7},{7,6},{8,9},{9,8},{10,11... | collective-permute-start | bytes 2064392 | tf_op jit(solution)/shard_map/ppermute | solution.py:916
  65.8 5.4 %copy-start.2 = (bf16[448,768]{1,0:T(8,128)(2,1)}, bf16[448,768]{1,0:T(8,128)(2,1)S(1)}, u32[]{:S(2)}) copy-start(bf16[448,768]{1,0:T(8,128)(2,1)S(1)} %collective-permute-done.5.refs_1_.refs_4_) | copy-start | bytes 2064388
  65.8 5.4 %collective-permute-start.8 = (bf16[448,768]{1,0:T(8,128)(2,1)S(1)}, bf16[448,768]{1,0:T(8,128)(2,1)S(1)}, u32[]{:S(2)}, u32[]{:S(2)}) collective-permute-start(bf16[448,768]{1,0:T(8,128)(2,1)S(1)} %collective-permute-done.5.refs_1_.refs_4_), channel_id=1, source_target_pairs={{0,1},{1,0},{2,3},{3,2},{4,5},{5,4},{6,7},{7,6},{8,9},{9,8},{10,11... | collective-permute-start | bytes 2064392 | tf_op jit(solution)/shard_map/ppermute | solution.py:916
  70.2 2.1 collective-permute-start.10
  230.7 10.4 %copy-start.30 = (f32[8,768]{1,0:T(8,128)S(1)}, f32[8,768]{1,0:T(8,128)}, u32[]{:S(2)}) copy-start(f32[8,768]{1,0:T(8,128)} %get-tuple-element.123) | copy-start | bytes 73732
  230.7 10.4 %copy-start.31 = (f32[4,768]{1,0:T(4,128)S(1)}, f32[4,768]{1,0:T(4,128)}, u32[]{:S(2)}) copy-start(f32[4,768]{1,0:T(4,128)} %get-tuple-element.125) | copy-start | bytes 36868
  230.8 10.5 %copy-start.28 = (f32[10,768]{1,0:T(8,128)S(1)}, f32[10,768]{1,0:T(8,128)}, u32[]{:S(2)}) copy-start(f32[10,768]{1,0:T(8,128)} %get-tuple-element.124) | copy-start | bytes 92164
  241.0 17.6 %collective-permute-start.11 = (bf16[2,768,768]{2,1,0:T(8,128)(2,1)}, bf16[2,768,768]{2,1,0:T(8,128)(2,1)}, u32[]{:S(2)}, u32[]{:S(2)}) collective-permute-start(bf16[2,768,768]{2,1,0:T(8,128)(2,1)} %shard_map.164), channel_id=1, source_target_pairs={{0,1},{1,0},{2,3},{3,2},{4,5},{5,4},{6,7},{7,6},{8,9},{9,8},{10,11... | collective-permute-start | bytes 7077896 | tf_op jit(solution)/shard_map/ppermute | solution.py:916
  258.6 28.2 %collective-permute-start.14 = (bf16[2,8,112,768]{3,2,1,0:T(8,128)(2,1)}, bf16[2,8,112,768]{3,2,1,0:T(8,128)(2,1)}, u32[]{:S(2)}, u32[]{:S(2)}) collective-permute-start(bf16[2,8,112,768]{3,2,1,0:T(8,128)(2,1)} %get-tuple-element.132), channel_id=1, source_target_pairs={{0,1},{1,0},{2,3},{3,2},{4,5},{5,4},{6,7},{7,6},{8,9},{9,8},{10,11... | collective-permute-start | bytes 8257544 | tf_op jit(solution)/shard_map/ppermute | solution.py:916
  262.9 23.9 %collective-permute-start.12 = (bf16[2,2,96,768]{3,2,1,0:T(8,128)(2,1)}, bf16[2,2,96,768]{3,2,1,0:T(8,128)(2,1)S(1)}, u32[]{:S(2)}, u32[]{:S(2)}) collective-permute-start(bf16[2,2,96,768]{3,2,1,0:T(8,128)(2,1)} %get-tuple-element.130), channel_id=1, source_target_pairs={{0,4},{4,0},{1,5},{5,1},{2,6},{6,2},{3,7},{7,3},{8,12},{12,8},{9,1... | collective-permute-start | bytes 1769480 | tf_op jit(solution)/shard_map/ppermute | solution.py:916
  264.6 22.2 %collective-permute-start.13 = (bf16[2,2,96,768]{3,2,1,0:T(8,128)(2,1)}, bf16[2,2,96,768]{3,2,1,0:T(8,128)(2,1)S(1)}, u32[]{:S(2)}, u32[]{:S(2)}) collective-permute-start(bf16[2,2,96,768]{3,2,1,0:T(8,128)(2,1)} %get-tuple-element.131), channel_id=1, source_target_pairs={{0,2},{2,0},{1,3},{3,1},{4,6},{6,4},{5,7},{7,5},{8,10},{10,8},{9,1... | collective-permute-start | bytes 1769480 | tf_op jit(solution)/shard_map/ppermute | solution.py:916
  286.8 29.4 %collective-permute-start.19 = (bf16[4,4,96,768]{3,2,1,0:T(8,128)(2,1)}, bf16[4,4,96,768]{3,2,1,0:T(8,128)(2,1)}, u32[]{:S(2)}, u32[]{:S(2)}) collective-permute-start(bf16[4,4,96,768]{3,2,1,0:T(8,128)(2,1)} %get-tuple-element.149), channel_id=1, source_target_pairs={{0,1},{1,0},{2,3},{3,2},{4,5},{5,4},{6,7},{7,6},{8,9},{9,8},{10,11... | collective-permute-start | bytes 7077896 | tf_op jit(solution)/shard_map/ppermute | solution.py:916
  292.0 24.2 %collective-permute-start.17 = (bf16[2,2,112,768]{3,2,1,0:T(8,128)(2,1)}, bf16[2,2,112,768]{3,2,1,0:T(8,128)(2,1)S(1)}, u32[]{:S(2)}, u32[]{:S(2)}) collective-permute-start(bf16[2,2,112,768]{3,2,1,0:T(8,128)(2,1)} %get-tuple-element.147), channel_id=1, source_target_pairs={{0,4},{4,0},{1,5},{5,1},{2,6},{6,2},{3,7},{7,3},{8,12},{12,8},{9,1... | collective-permute-start | bytes 2064392 | tf_op jit(solution)/shard_map/ppermute | solution.py:916
  292.9 23.3 %collective-permute-start.18 = (bf16[2,2,112,768]{3,2,1,0:T(8,128)(2,1)}, bf16[2,2,112,768]{3,2,1,0:T(8,128)(2,1)S(1)}, u32[]{:S(2)}, u32[]{:S(2)}) collective-permute-start(bf16[2,2,112,768]{3,2,1,0:T(8,128)(2,1)} %get-tuple-element.148), channel_id=1, source_target_pairs={{0,2},{2,0},{1,3},{3,1},{4,6},{6,4},{5,7},{7,5},{8,10},{10,8},{9,1... | collective-permute-start | bytes 2064392 | tf_op jit(solution)/shard_map/ppermute | solution.py:916
  294.1 22.1 %collective-permute-start.15 = (bf16[2,96,768]{2,1,0:T(8,128)(2,1)}, bf16[2,96,768]{2,1,0:T(8,128)(2,1)S(1)}, u32[]{:S(2)}, u32[]{:S(2)}) collective-permute-start(bf16[2,96,768]{2,1,0:T(8,128)(2,1)} %get-tuple-element.145), channel_id=1, source_target_pairs={{0,2},{2,0},{1,3},{3,1},{4,6},{6,4},{5,7},{7,5},{8,10},{10,8},{9,1... | collective-permute-start | bytes 884744 | tf_op jit(solution)/shard_map/ppermute | solution.py:916
  294.9 21.3 %collective-permute-start.16 = (bf16[2,96,768]{2,1,0:T(8,128)(2,1)}, bf16[2,96,768]{2,1,0:T(8,128)(2,1)S(1)}, u32[]{:S(2)}, u32[]{:S(2)}) collective-permute-start(bf16[2,96,768]{2,1,0:T(8,128)(2,1)} %get-tuple-element.146), channel_id=1, source_target_pairs={{0,4},{4,0},{1,5},{5,1},{2,6},{6,2},{3,7},{7,3},{8,12},{12,8},{9,1... | collective-permute-start | bytes 884744 | tf_op jit(solution)/shard_map/ppermute | solution.py:916
  321.8 22.3 %collective-permute-start.23 = (bf16[2,2,96,768]{3,2,1,0:T(8,128)(2,1)}, bf16[2,2,96,768]{3,2,1,0:T(8,128)(2,1)S(1)}, u32[]{:S(2)}, u32[]{:S(2)}) collective-permute-start(bf16[2,2,96,768]{3,2,1,0:T(8,128)(2,1)} %get-tuple-element.160), channel_id=1, source_target_pairs={{0,4},{4,0},{1,5},{5,1},{2,6},{6,2},{3,7},{7,3},{8,12},{12,8},{9,1... | collective-permute-start | bytes 1769480 | tf_op jit(solution)/shard_map/ppermute | solution.py:916
  323.1 21.1 %collective-permute-start.24 = (bf16[2,2,96,768]{3,2,1,0:T(8,128)(2,1)}, bf16[2,2,96,768]{3,2,1,0:T(8,128)(2,1)S(1)}, u32[]{:S(2)}, u32[]{:S(2)}) collective-permute-start(bf16[2,2,96,768]{3,2,1,0:T(8,128)(2,1)} %get-tuple-element.161), channel_id=1, source_target_pairs={{0,2},{2,0},{1,3},{3,1},{4,6},{6,4},{5,7},{7,5},{8,10},{10,8},{9,1... | collective-permute-start | bytes 1769480 | tf_op jit(solution)/shard_map/ppermute | solution.py:916
  324.7 19.4 %collective-permute-start.21 = (bf16[2,112,768]{2,1,0:T(8,128)(2,1)}, bf16[2,112,768]{2,1,0:T(8,128)(2,1)S(1)}, u32[]{:S(2)}, u32[]{:S(2)}) collective-permute-start(bf16[2,112,768]{2,1,0:T(8,128)(2,1)} %get-tuple-element.158), channel_id=1, source_target_pairs={{0,2},{2,0},{1,3},{3,1},{4,6},{6,4},{5,7},{7,5},{8,10},{10,8},{9,1... | collective-permute-start | bytes 1032200 | tf_op jit(solution)/shard_map/ppermute | solution.py:916
  325.1 19.0 %collective-permute-start.22 = (bf16[2,112,768]{2,1,0:T(8,128)(2,1)}, bf16[2,112,768]{2,1,0:T(8,128)(2,1)S(1)}, u32[]{:S(2)}, u32[]{:S(2)}) collective-permute-start(bf16[2,112,768]{2,1,0:T(8,128)(2,1)} %get-tuple-element.159), channel_id=1, source_target_pairs={{0,4},{4,0},{1,5},{5,1},{2,6},{6,2},{3,7},{7,3},{8,12},{12,8},{9,1... | collective-permute-start | bytes 1032200 | tf_op jit(solution)/shard_map/ppermute | solution.py:916
  325.9 8.2 %collective-permute-start.20 = (bf16[96,768]{1,0:T(8,128)(2,1)}, bf16[96,768]{1,0:T(8,128)(2,1)S(1)}, u32[]{:S(2)}, u32[]{:S(2)}) collective-permute-start(bf16[96,768]{1,0:T(8,128)(2,1)} %get-tuple-element.157), channel_id=1, source_target_pairs={{0,16},{8,24},{16,0},{24,8},{1,17},{9,25},{17,1},{25,9},{2,18},{10... | collective-permute-start | bytes 442376 | tf_op jit(solution)/shard_map/ppermute | solution.py:916
  334.2 10.0 %copy-start.25 = (bf16[96,768]{1,0:T(8,128)(2,1)}, bf16[96,768]{1,0:T(8,128)(2,1)S(1)}, u32[]{:S(2)}) copy-start(bf16[96,768]{1,0:T(8,128)(2,1)S(1)} %collective-permute-done.20) | copy-start | bytes 442372
  345.4 10.5 %copy-start.27 = (f32[10,768]{1,0:T(8,128)S(1)}, f32[10,768]{1,0:T(8,128)}, u32[]{:S(2)}) copy-start(f32[10,768]{1,0:T(8,128)} %get-tuple-element.176) | copy-start | bytes 92164
  350.2 22.6 %collective-permute-start.25 = (bf16[208,768]{1,0:T(8,128)(2,1)}, bf16[208,768]{1,0:T(8,128)(2,1)S(1)}, u32[]{:S(2)}, u32[]{:S(2)}) collective-permute-start(bf16[208,768]{1,0:T(8,128)(2,1)} %get-tuple-element.168), channel_id=1, source_target_pairs={{0,8},{8,0},{16,24},{24,16},{1,9},{9,1},{17,25},{25,17},{2,10},{10... | collective-permute-start | bytes 958472 | tf_op jit(solution)/shard_map/ppermute | solution.py:916
  350.3 22.6 %collective-permute-start.26 = (bf16[208,768]{1,0:T(8,128)(2,1)}, bf16[208,768]{1,0:T(8,128)(2,1)S(1)}, u32[]{:S(2)}, u32[]{:S(2)}) collective-permute-start(bf16[208,768]{1,0:T(8,128)(2,1)} %get-tuple-element.169), channel_id=1, source_target_pairs={{0,24},{8,16},{16,8},{24,0},{1,25},{9,17},{17,9},{25,1},{2,26},{10... | collective-permute-start | bytes 958472 | tf_op jit(solution)/shard_map/ppermute | solution.py:916
  353.1 19.7 %collective-permute-start.28 = (bf16[2,96,768]{2,1,0:T(8,128)(2,1)}, bf16[2,96,768]{2,1,0:T(8,128)(2,1)S(1)}, u32[]{:S(2)}, u32[]{:S(2)}) collective-permute-start(bf16[2,96,768]{2,1,0:T(8,128)(2,1)} %get-tuple-element.171), channel_id=1, source_target_pairs={{0,2},{2,0},{1,3},{3,1},{4,6},{6,4},{5,7},{7,5},{8,10},{10,8},{9,1... | collective-permute-start | bytes 884744 | tf_op jit(solution)/shard_map/ppermute | solution.py:916
  354.8 17.9 %collective-permute-start.29 = (bf16[2,96,768]{2,1,0:T(8,128)(2,1)}, bf16[2,96,768]{2,1,0:T(8,128)(2,1)S(1)}, u32[]{:S(2)}, u32[]{:S(2)}) collective-permute-start(bf16[2,96,768]{2,1,0:T(8,128)(2,1)} %get-tuple-element.172), channel_id=1, source_target_pairs={{0,4},{4,0},{1,5},{5,1},{2,6},{6,2},{3,7},{7,3},{8,12},{12,8},{9,1... | collective-permute-start | bytes 884744 | tf_op jit(solution)/shard_map/ppermute | solution.py:916
  355.4 17.4 %collective-permute-start.27 = (bf16[112,768]{1,0:T(8,128)(2,1)}, bf16[112,768]{1,0:T(8,128)(2,1)S(1)}, u32[]{:S(2)}, u32[]{:S(2)}) collective-permute-start(bf16[112,768]{1,0:T(8,128)(2,1)} %get-tuple-element.170), channel_id=1, source_target_pairs={{0,16},{8,24},{16,0},{24,8},{1,17},{9,25},{17,1},{25,9},{2,18},{10... | collective-permute-start | bytes 516104 | tf_op jit(solution)/shard_map/ppermute | solution.py:916
  356.5 16.3 %copy-start.23 = (bf16[112,768]{1,0:T(8,128)(2,1)S(1)}, bf16[112,768]{1,0:T(8,128)(2,1)}, u32[]{:S(2)}) copy-start(bf16[112,768]{1,0:T(8,128)(2,1)} %get-tuple-element.184) | copy-start | bytes 516100
  373.9 8.4 %copy-start.24 = (bf16[96,768]{1,0:T(8,128)(2,1)S(1)}, bf16[96,768]{1,0:T(8,128)(2,1)}, u32[]{:S(2)}) copy-start(bf16[96,768]{1,0:T(8,128)(2,1)} %get-tuple-element.188) | copy-start | bytes 442372
  373.9 8.4 %copy-start.26 = (bf16[96,768]{1,0:T(8,128)(2,1)S(1)}, bf16[96,768]{1,0:T(8,128)(2,1)}, u32[]{:S(2)}) copy-start(bf16[96,768]{1,0:T(8,128)(2,1)} %copy-done.25) | copy-start | bytes 442372
  377.3 7.8 %collective-permute-start.30 = (bf16[96,768]{1,0:T(8,128)(2,1)}, bf16[96,768]{1,0:T(8,128)(2,1)S(1)}, u32[]{:S(2)}, u32[]{:S(2)}) collective-permute-start(bf16[96,768]{1,0:T(8,128)(2,1)} %get-tuple-element.181), channel_id=1, source_target_pairs={{0,8},{8,0},{16,24},{24,16},{1,9},{9,1},{17,25},{25,17},{2,10},{10... | collective-permute-start | bytes 442376 | tf_op jit(solution)/shard_map/ppermute | solution.py:916
  377.4 12.1 %collective-permute-start.31 = (bf16[96,768]{1,0:T(8,128)(2,1)}, bf16[96,768]{1,0:T(8,128)(2,1)S(1)}, u32[]{:S(2)}, u32[]{:S(2)}) collective-permute-start(bf16[96,768]{1,0:T(8,128)(2,1)} %get-tuple-element.182), channel_id=1, source_target_pairs={{0,16},{8,24},{16,0},{24,8},{1,17},{9,25},{17,1},{25,9},{2,18},{10... | collective-permute-start | bytes 442376 | tf_op jit(solution)/shard_map/ppermute | solution.py:916
  380.5 8.9 %collective-permute-start.32 = (bf16[96,768]{1,0:T(8,128)(2,1)}, bf16[96,768]{1,0:T(8,128)(2,1)S(1)}, u32[]{:S(2)}, u32[]{:S(2)}) collective-permute-start(bf16[96,768]{1,0:T(8,128)(2,1)} %get-tuple-element.183), channel_id=1, source_target_pairs={{0,24},{8,16},{16,8},{24,0},{1,25},{9,17},{17,9},{25,1},{2,26},{10... | collective-permute-start | bytes 442376 | tf_op jit(solution)/shard_map/ppermute | solution.py:916
  (18 other events, 20.7 us)
Sparse Core Ops, SparseCore 0:
  11.5 92.6 all-gather.1
